TPU v7x, 256 devices: a whole 4x4x8 slice. The times are simulated.
256 devices in a mesh: replica: 8 (over x, core), tensor: 32 (over y, z).
Axes of the slice: x: 4, y: 4, z: 8, core: 2. Of those that a mesh axis runs over, the one named last changes fastest.
Arguments:
- kv_pool: bfloat16 [8, 512, 32, 2048], P('replica', 'tensor'), may hold values from -6 to 6
- page_table: int32 [8, 4, 128], P('replica', None, 'tensor'), may hold values from 0 to 15, as said below
- lengths: int32 [8, 4], replicated, may hold values from 1 to 4096, as said below
- steal_plan: int32 [8, 3, 2], replicated, may hold values from 0 to 7, as said below
- hidden_rows: bfloat16 [8, 2, 7, 16384], P('replica', None, None, 'tensor'), may hold values from -6 to 6
- kv_weight: bfloat16 [16384, 2048], P('tensor'), may hold values from -0.046875 to 0.046875
- queries: bfloat16 [8, 2, 7, 16384], P('replica', None, None, 'tensor'), may hold values from -300 to 300
Outputs:
- attended: bfloat16 [8, 2, 7, 16384], P('replica', None, None, 'tensor')
Inputs may be any that keep to these rules, and one draw needn't show every extreme that they name: `page_table`: on each tensor device t, columns t * 4 to t * 4 + 3 of all 4 requests of a replica name each of its 16 slots once. `lengths`: every replica holds a request of exactly 4096 tokens. `steal_plan`: in row d the source replica is never d; each source named in a row is named exactly 1 times, in consecutive entries.
All inputs are finite; a program needn't handle non-finite values. Where the computation divides by a largest or mean magnitude, that divisor is 1e-20 or more.
Results may differ from a plain program's by a relative error of at most 0.039.
Values may be sent and summed in bfloat16 or wider, within the bound.
A program may use at most 128 MiB of HBM per device.

v0:
```python
import math

import jax
import jax.numpy as jnp
from jax import lax
from jax.sharding import PartitionSpec as P

QH = 128
KVH = 8
HD = 128
PAGE = 32
PPD = 4
CAP = 1
STEAL_IN = 3


masked_score = -1e30


def joined(array, axis, combine):
    everything = jax.tree.map(lambda part: lax.all_gather(part, axis), array)
    first = jax.tree.map(lambda part: part[0], everything)

    def step(k, so_far):
        return combine(so_far, jax.tree.map(lambda part: part[k], everything))

    return lax.fori_loop(1, lax.axis_size(axis), step, first)


def hadamard(order):
    counter = jnp.arange(order, dtype=jnp.int32)
    intersection = jnp.bitwise_and(counter[:, None], counter[None, :])
    parity = jnp.zeros((order, order), jnp.int32)
    for bit_index in range(order.bit_length() - 1):
        parity = parity + jnp.bitwise_and(jnp.right_shift(intersection, bit_index), 1)
    signs = 1.0 - 2.0 * jnp.bitwise_and(parity, 1).astype(jnp.float32)
    return signs / math.sqrt(order)


def rotate_pack(leaving, rotation):
    shaped = leaving.astype(jnp.float32).reshape(leaving.shape[:-1] + (2 * KVH, HD))
    turned = jnp.einsum("...d,de->...e", shaped, rotation, precision=lax.Precision.HIGHEST)
    scales = lax.optimization_barrier(
        (jnp.max(jnp.abs(turned), axis=-1) + 1e-06).astype(jnp.bfloat16)
    )
    packed = (turned / scales.astype(jnp.float32)[..., None]).astype(jnp.bfloat16)
    return (packed.reshape(leaving.shape), scales)


def unpack(packed, scales, rotation):
    shaped = packed.astype(jnp.float32).reshape(packed.shape[:-1] + (2 * KVH, HD))
    shaped = shaped * scales.astype(jnp.float32)[..., None]
    back = jnp.einsum("...d,de->...e", shaped, rotation, precision=lax.Precision.HIGHEST)
    return back.reshape(packed.shape).astype(jnp.bfloat16)


def local_attention(every_query, keys, fresh, key_valid, tail_valid):
    rows_all = keys.shape[0]
    group = QH // KVH
    query = every_query.reshape(2, rows_all, KVH, group, HD)
    key_part = keys[..., : KVH * HD].reshape(rows_all, -1, KVH, HD)
    value_part = keys[..., KVH * HD :].reshape(rows_all, -1, KVH, HD)
    new_keys = fresh[..., : KVH * HD].reshape(2, rows_all, KVH, HD)
    new_values = fresh[..., KVH * HD :].reshape(2, rows_all, KVH, HD)
    factor = 1.0 / math.sqrt(HD)
    score = (
        jnp.einsum("srkgd,rlkd->srkgl", query, key_part, preferred_element_type=jnp.float32)
        * factor
    )
    score = jnp.where(key_valid[None, :, None, None, :], score, masked_score)
    tail = (
        jnp.einsum("srkgd,trkd->srkgt", query, new_keys, preferred_element_type=jnp.float32)
        * factor
    )
    tail = jnp.where(tail_valid[:, :, None, None, :], tail, masked_score)
    top = jnp.maximum(jnp.max(score, axis=-1), jnp.max(tail, axis=-1))
    weights = jnp.exp(score - top[..., None])
    tail_weights = jnp.exp(tail - top[..., None])
    total = jnp.sum(weights, axis=-1) + jnp.sum(tail_weights, axis=-1)
    mixed = jnp.einsum(
        "srkgl,rlkd->srkgd",
        weights.astype(jnp.bfloat16),
        value_part,
        preferred_element_type=jnp.float32,
    )
    mixed = mixed + jnp.einsum(
        "srkgt,trkd->srkgd",
        tail_weights.astype(jnp.bfloat16),
        new_values,
        preferred_element_type=jnp.float32,
    )
    return (top, total, mixed)


def combine_partials(first, second):
    peak = jnp.maximum(first[0], second[0])
    first_factor = jnp.exp(first[0] - peak)
    second_factor = jnp.exp(second[0] - peak)
    summed = first[1] * first_factor + second[1] * second_factor
    weighted = first[2] * first_factor[..., None] + second[2] * second_factor[..., None]
    return (peak, summed, weighted)


def build_masks(spans, tparts, tensor_index):
    page_index = jnp.arange(PPD, dtype=jnp.int32)[:, None]
    token_index = jnp.arange(PAGE, dtype=jnp.int32)[None, :]
    key_position = ((page_index * tparts + tensor_index) * PAGE + token_index).reshape(-1)
    key_valid = key_position[None, :] < spans[:, None]
    step_index = jnp.arange(2, dtype=jnp.int32)
    owner = (spans[None, :] + step_index[:, None]) // PAGE % tparts == tensor_index
    tail_valid = (step_index[None, :] <= step_index[:, None])[:, None, :] & jnp.transpose(owner)[
        None, :, :
    ]
    return (key_valid, tail_valid)


def on_device(kv_pool, page_table, lengths, steal_plan, hidden_rows, kv_weight, queries):
    groups = lax.axis_size("replica")
    tparts = lax.axis_size("tensor")
    replica_index = lax.axis_index("replica")
    tensor_index = lax.axis_index("tensor")
    rotation = hadamard(HD)
    width = kv_pool.shape[-1]
    pool = kv_pool[0]
    local_table = page_table[0]
    rows_here = local_table.shape[0]
    rows_all = rows_here + STEAL_IN
    slot_count = groups * CAP
    partial_value = jnp.einsum(
        "srd,de->sre", hidden_rows[0], kv_weight, preferred_element_type=jnp.float32
    )
    fresh = lax.psum(partial_value.astype(jnp.bfloat16), "tensor")
    every_query = lax.all_gather(queries[0], "tensor", axis=2, tiled=True)
    sources = steal_plan[:, :, 0]
    requested = steal_plan[:, :, 1]
    from_here = (sources == replica_index).astype(jnp.int32)
    earlier = jnp.cumsum(from_here, axis=1) - from_here
    target = jnp.arange(groups, dtype=jnp.int32)[:, None] * CAP + earlier
    outgoing = jnp.arange(slot_count, dtype=jnp.int32)
    matched = (target[None] == outgoing[:, None, None]) & (from_here[None] == 1)
    chosen = jnp.sum(jnp.where(matched, requested[None], 0), axis=(1, 2))
    leaving_slots = jnp.take(local_table, chosen, axis=0).reshape(-1)
    leaving = jnp.take(pool, leaving_slots, axis=0).reshape(slot_count, PPD, PAGE, width)
    packed, scales = rotate_pack(leaving, rotation)
    my_sources = lax.dynamic_index_in_dim(sources, replica_index, 0, keepdims=False)
    my_requests = lax.dynamic_index_in_dim(requested, replica_index, 0, keepdims=False)
    entry_index = jnp.arange(STEAL_IN, dtype=jnp.int32)
    before = (my_sources[:, None] == my_sources[None, :]) & (
        entry_index[None, :] < entry_index[:, None]
    )
    landing = my_sources * CAP + jnp.sum(before.astype(jnp.int32), axis=1)
    resident = jnp.take(pool, local_table.reshape(-1), axis=0).reshape(rows_here, PPD * PAGE, width)
    own_lengths = lax.dynamic_index_in_dim(lengths, replica_index, 0, keepdims=False)
    arrived, arrived_scales = (
        lax.all_to_all(packed, "replica", split_axis=0, concat_axis=0, tiled=True),
        lax.all_to_all(scales, "replica", split_axis=0, concat_axis=0, tiled=True),
    )
    stolen = unpack(
        jnp.take(arrived, landing, axis=0), jnp.take(arrived_scales, landing, axis=0), rotation
    )
    keys = jnp.concatenate([resident, stolen.reshape(STEAL_IN, PPD * PAGE, width)], axis=0)
    spans = jnp.concatenate([own_lengths, lengths[my_sources, my_requests]])
    key_valid, tail_valid = build_masks(spans, tparts, tensor_index)
    top, total, mixed = local_attention(every_query, keys, fresh, key_valid, tail_valid)
    heads_here = QH // tparts
    top, total, mixed = joined((top, total, mixed), "tensor", combine_partials)
    mine_total = lax.dynamic_slice_in_dim(
        total.reshape(2, rows_all, QH), tensor_index * heads_here, heads_here, 2
    )
    mine_mixed = lax.dynamic_slice_in_dim(
        mixed.reshape(2, rows_all, QH, HD), tensor_index * heads_here, heads_here, 2
    )
    result = (mine_mixed / mine_total[..., None]).reshape(2, rows_all, heads_here * HD)
    return result[None].astype(jnp.bfloat16)


def solution(mesh):
    return jax.shard_map(
        on_device,
        mesh=mesh,
        in_specs=(
            P("replica", "tensor", None, None),
            P("replica", None, "tensor"),
            P(),
            P(),
            P("replica", None, None, "tensor"),
            P("tensor", None),
            P("replica", None, None, "tensor"),
        ),
        out_specs=P("replica", None, None, "tensor"),
        check_vma=False,
    )
```

profile of v0, /device:TPU:1, one launch (start us, length us, event | category | flops | bytes accessed | tf_op | source)
XLA Modules:
  0.0 592.2 jit_solution(5954607895948494224)
XLA Ops:
  9.8 2.7 gather_fusion.3
  12.5 3.6 copy.145
  16.1 5.8 abs_reduce_fusion
  22.9 6.5 %all-to-all-start.1 = ((bf16[8,2,1024]{2,1,0:T(2,128)(2,1)}), bf16[8,2,1024]{2,1,0:T(2,128)(2,1)S(1)}, u32[]{:S(2)}, u32[]{:S(2)}) async-start(bf16[8,2,1024]{2,1,0:T(2,128)(2,1)} %reshape.494), calls=%async_computation.1 | async-start | bytes 65536 | tf_op jit(solution)/shard_map/all_to_all | solution.py:156
  29.5 6.9 %divide_convert_fusion = bf16[8,4,32,16,128]{4,3,2,1,0:T(8,128)(2,1)} fusion(f32[8,4,32,16,128]{4,3,2,1,0:T(8,128)} %get-tuple-element.255, f32[8,4,32,16]{3,2,1,0:T(8,128)S(1)} %convert_element_type.81), kind=kLoop, calls=%fused_computation.16 | loop fusion | flops 4194304 | bytes 12648448 | tf_op jit(solution)/shard_map/convert_element_type | solution.py:46
  36.3 7.3 %reshape.415 = bf16[8,4,32,2048]{3,2,1,0:T(8,128)(2,1)} reshape(bf16[8,4,32,16,128]{4,3,2,1,0:T(8,128)(2,1)} %divide_convert_fusion) | data formatting | bytes 8388608 | tf_op jit(solution)/shard_map/reshape | solution.py:47
  43.7 5.0 all-to-all-start
  50.4 2.0 convolution_convert_fusion
  52.4 117.7 %psum.7 = bf16[2,7,2048]{2,1,0:T(8,128)(2,1)S(1)} all-reduce(bf16[2,7,2048]{2,1,0:T(8,128)(2,1)S(1)} %convolution_convert_fusion), channel_id=1, replica_groups=mesh['replica'=8,'tensor'=32] {'tensor'}, use_global_device_ids=true, to_apply=%region_5.6 | all-reduce | flops 28672 | bytes 114688 | tf_op jit(solution)/shard_map/psum | solution.py:132
  170.2 35.5 %all-gather = bf16[1,2,7,16384]{3,1,2,0:T(2,128)(2,1)S(1)} all-gather(bf16[1,2,7,512]{3,1,2,0:T(2,128)(2,1)S(1)} %copy-done.9), channel_id=2, replica_groups=mesh['replica'=8,'tensor'=32] {'tensor'}, dimensions={3}, use_global_device_ids=true | all-gather | bytes 473088 | tf_op jit(solution)/shard_map/all_gather | solution.py:133
  206.1 2.1 gather_fusion.1
  209.6 1.8 bitcast_select_fusion
  212.4 4.0 gather_fusion.4
  216.4 1.8 copy.146
  218.2 3.9 fusion.13
  222.1 3.7 convert_element_type.86
  225.8 3.2 pad_maximum_fusion
  229.0 3.9 copy.114
  232.9 2.5 copy.105
  235.4 2.3 fusion.84
  241.2 38.0 %all-gather.1 = f32[64,7,8,16]{3,2,1,0:T(8,128)S(1)} all-gather(f32[2,7,8,16]{3,2,1,0:T(8,128)S(1)} %copy.112), channel_id=3, replica_groups=mesh['replica'=8,'tensor'=32] {'tensor'}, dimensions={0}, use_global_device_ids=true | all-gather | bytes 236544 | tf_op jit(solution)/shard_map/all_gather | solution.py:21
  279.2 43.4 %all-gather.2 = f32[64,7,8,16]{3,2,1,0:T(8,128)S(1)} all-gather(f32[2,7,8,16]{3,2,1,0:T(8,128)S(1)} %copy.113), channel_id=4, replica_groups=mesh['replica'=8,'tensor'=32] {'tensor'}, dimensions={0}, use_global_device_ids=true | all-gather | bytes 236544 | tf_op jit(solution)/shard_map/all_gather | solution.py:21
  323.9 173.8 %all-gather.6.cloned.1.call-done = f32[64,7,8,16,128]{4,3,0,2,1:T(8,128)} async-done(((f32[2,7,8,16,128]{4,3,0,2,1:T(8,128)}), f32[64,7,8,16,128]{4,3,0,2,1:T(8,128)}) %all-gather.6.cloned.1.call-update) | async-done | bytes 29360144 | tf_op jit(solution)/shard_map/all_gather | solution.py:21
  499.0 84.7 %while.19 = (s32[]{:T(128)}, f32[2,7,8,16]{3,2,1,0:T(8,128)S(1)}, f32[2,7,8,16]{3,2,1,0:T(8,128)S(1)}, f32[2,7,8,16,128]{4,3,2,1,0:T(8,128)S(1)}, f32[32,2,7,8,1...) while((s32[]{:T(128)}, f32[2,7,8,16]{3,2,1,0:T(8,128)S(1)}, ...), condition=%wide.region_10.11_spmd, body=%wide.region_9.10_spmd.sunk | while | flops 698885 | bytes 2824335 | solution.py:27
  500.0 1.8 fusion.91
  502.7 1.8 fusion.91
  505.4 1.8 fusion.91
  508.2 1.8 fusion.91
  510.9 1.8 fusion.91
  513.6 1.8 fusion.91
  516.4 1.8 fusion.91
  519.1 1.8 fusion.91
  521.8 1.8 fusion.91
  524.6 1.8 fusion.91
  527.3 1.8 fusion.91
  530.0 1.8 fusion.91
  532.8 1.8 fusion.91
  535.5 1.8 fusion.91
  538.2 1.8 fusion.91
  541.0 1.8 fusion.91
  543.7 1.8 fusion.91
  546.4 1.8 fusion.91
  549.1 1.8 fusion.91
  551.9 1.8 fusion.91
  554.6 1.8 fusion.91
  557.3 1.8 fusion.91
  560.1 1.8 fusion.91
  562.8 1.8 fusion.91
  (130 shorter events, 57.3 us)
Async XLA Ops:
  6.5 3.2 copy-start
  16.1 13.3 %copy-start.7 = (s32[1,4,4]{2,1,0:T(4,128)S(1)}, s32[1,4,4]{2,1,0:T(4,128)}, u32[]{:S(2)}) copy-start(s32[1,4,4]{2,1,0:T(4,128)} %param.10) | copy-start | bytes 196
  22.9 20.7 %all-to-all-start.1 = ((bf16[8,2,1024]{2,1,0:T(2,128)(2,1)}), bf16[8,2,1024]{2,1,0:T(2,128)(2,1)S(1)}, u32[]{:S(2)}, u32[]{:S(2)}) async-start(bf16[8,2,1024]{2,1,0:T(2,128)(2,1)} %reshape.494), calls=%async_computation.1 | async-start | bytes 65536 | tf_op jit(solution)/shard_map/all_to_all | solution.py:156
  43.7 5.4 copy-start.2
  43.7 6.7 %copy-start.8 = (bf16[1,2,7,512]{3,1,2,0:T(2,128)(2,1)S(1)}, bf16[1,2,7,512]{3,1,2,0:T(2,128)(2,1)}, u32[]{:S(2)}) copy-start(bf16[1,2,7,512]{3,1,2,0:T(2,128)(2,1)} %param.13) | copy-start | bytes 43012
  43.7 168.7 %all-to-all-start = ((bf16[8,4,32,2048]{3,2,1,0:T(8,128)(2,1)}), bf16[8,4,32,2048]{3,2,1,0:T(8,128)(2,1)}, u32[]{:S(2)}, u32[]{:S(2)}) async-start(bf16[8,4,32,2048]{3,2,1,0:T(8,128)(2,1)} %reshape.415), calls=%async_computation | async-start | bytes 8388608 | tf_op jit(solution)/shard_map/all_to_all | solution.py:155
  48.6 121.6 %copy-start.9 = (bf16[1,2,7,512]{3,1,2,0:T(2,128)(2,1)S(1)}, bf16[1,2,7,512]{3,1,2,0:T(2,128)(2,1)}, u32[]{:S(2)}) copy-start(bf16[1,2,7,512]{3,1,2,0:T(2,128)(2,1)} %param.15) | copy-start | bytes 43012
  48.6 449.1 %all-gather.6.cloned.1.call-start = ((), (), s32[]{:S(2)}) async-start(), calls=%async_computation.2 | async-start | bytes 30277632 | tf_op jit(solution)/shard_map/all_gather | solution.py:21
  229.0 3.9 copy-start.3
  235.4 2.4 copy-start.6
  279.2 44.7 %copy-start.4 = (f32[64,7,8,16]{3,2,1,0:T(8,128)}, f32[64,7,8,16]{3,2,1,0:T(8,128)S(1)}, u32[]{:S(2)}) copy-start(f32[64,7,8,16]{3,2,1,0:T(8,128)S(1)} %all-gather.1) | copy-start | bytes 688132
  322.7 1.3 copy-start.5
  497.8 1.2 slice-start
  583.7 1.6 copy-start.1
Sparse Core Ops, SparseCore 0:
  240.4 257.3 all-gather.5
where the time goes:
time: 596 us; the launch traced here: 592 us
  blocking collectives  235 us (39%)
  waiting for transfers between devices  174 us (29%)
  other arithmetic  98.7 us (17%)
  local copies, waits for them, and re-layouts  41.4 us (7%)
  matrix products  17.7 us (3%)
  between operations  13.7 us (2%)
  starting transfers between devices  11.4 us (2%)
    all_gather x1, waiting for transfers between devices, joined(): everything = jax.tree.map(lambda part: lax.all_gather(part, axis), array)  174 us
    psum x1, blocking collectives, on_device(): fresh = lax.psum(partial_value.astype(jnp.bfloat16), 'tensor')  118 us
    all_gather x2, blocking collectives, joined(): everything = jax.tree.map(lambda part: lax.all_gather(part, axis), array)  81.4 us
    add x31, other arithmetic, combine_partials(): first[2] * first_factor[..., None] + second[2] * second_factor[..., None]  55.6 us
    all_gather x1, blocking collectives, on_device(): every_query = lax.all_gather(queries[0], 'tensor', axis=2, tiled=True)  35.5 us
    add x31, other arithmetic, combine_partials(): summed = first[1] * first_factor + second[1] * second_factor  28.3 us
  transfers between devices with their start and end apart: 3, of which 1 were waited for; matrix products, arithmetic and copies ran while one was open for 4% of the time, Pallas kernels for 0%

commit v1 on v0

v1 whole, which is shorter than its diff:
```python
import functools
import math

import jax
import jax.numpy as jnp
from jax import lax
from jax.experimental import pallas as pl
from jax.experimental.pallas import tpu as pltpu
from jax.sharding import PartitionSpec as P

KVH = 8
HD = 128
PAGE = 32
PPD = 4
STEAL_IN = 3
ROWS = 4
ROWS_ALL = 7
SLOTS = 16
NR = 8
NY = 4
NZ = 8
NT = NY * NZ
MASKED = -1e30
MESH = pl.DeviceIdType.MESH
F32 = jnp.float32
BF16 = jnp.bfloat16
INV = 1.0 / math.sqrt(HD)
NPO = 2
NPS = 4


def lanes(shape):
    return lax.broadcasted_iota(jnp.int32, shape, len(shape) - 1)


def rolled(x, by):
    return pltpu.roll(x, by % 128, 1)


def halves(x):
    high = x.astype(BF16).astype(F32)
    return high, (x - high).astype(BF16).astype(F32)


def merged_stats(tiles, pairs):
    tops, totals = [], []
    for tile in tiles:
        both = tile + rolled(tile, -pairs)
        tops.append(both)
        totals.append(rolled(both, -2 * pairs))
    top = functools.reduce(jnp.maximum, tops)
    factors = [jnp.exp(one - top) for one in tops]
    total = sum(f * l for f, l in zip(factors, totals))
    return top, total, factors


def kernel(
    table, lengths, plan, q_ref, h_ref, pool_hbm, w_hbm, out_ref,
    pool, moved, w, qt, qo, qs, xsend, xrecv, fsend, frecv, fsum, fz, fresh,
    obo, obs, rbo, rbs, sto, sts, mbo, mbs, zbo, zbs, bsend, brecv, fin,
    lsem, ss, rs,
):
    me = lax.axis_index("replica")
    t = lax.axis_index("tensor")
    y, z = t // NZ, t % NZ
    ypeer = [None] + [(me, ((y + o) % NY) * NZ + z) for o in range(1, NY)]
    zpeer = [None] + [(me, y * NZ + (z + o) % NZ) for o in range(1, NZ)]
    xpeer = [None] + [((me + o) % NR, t) for o in range(1, NR)]
    zorder = (1, 7, 2, 6, 3, 5, 4)

    pool_copy = pltpu.make_async_copy(pool_hbm, pool, lsem.at[0])
    w_copy = pltpu.make_async_copy(w_hbm, w, lsem.at[1])
    w_copy.start()
    pool_copy.start()

    barrier = pltpu.get_barrier_semaphore()
    peers = zpeer[1:] + ypeer[1:] + xpeer[1:]
    for peer in peers:
        pl.semaphore_signal(barrier, inc=1, device_id=peer, device_id_type=MESH)

    for s in range(2):
        for j in range(4):
            qt[pl.ds(s * 4 + j, ROWS_ALL, stride=8), :] = q_ref[s, :, j * HD:(j + 1) * HD].astype(F32)
    qo[t] = qt[0:32].astype(BF16)
    for o in range(1, NR):
        source = (me + o) % NR
        chosen = jnp.zeros((8, HD), F32)
        for e in range(STEAL_IN):
            tile = qt[(ROWS + e) * 8:(ROWS + e + 1) * 8]
            chosen = chosen + jnp.where(plan[me, e, 0] == source, tile, 0.0)
        xsend[o] = chosen
    xrecv[me] = jnp.zeros((8, HD), F32)
    sto[...] = jnp.zeros_like(sto)
    sts[...] = jnp.zeros_like(sts)

    count = [0, 0]
    sends = []

    def fresh_index(kind, n=1):
        first = count[kind]
        count[kind] += n
        return first

    def push(src, dst, recv, peer):
        copy = pltpu.make_async_remote_copy(
            src_ref=src, dst_ref=dst, send_sem=ss.at[fresh_index(0)], recv_sem=rs.at[recv],
            device_id=peer, device_id_type=MESH,
        )
        copy.start()
        sends.append(copy)

    def arrive(dst, recv):
        pltpu.make_async_remote_copy(
            src_ref=dst, dst_ref=dst, send_sem=ss.at[0], recv_sem=rs.at[recv],
            device_id=xpeer[1], device_id_type=MESH,
        ).wait_recv()

    x_r = fresh_index(1, NR)
    qoz_r = fresh_index(1, NZ)
    qoy_r = fresh_index(1, NY)
    qsz_r = fresh_index(1, NZ)
    qsy_r = fresh_index(1, NY)
    fy_r = fresh_index(1, NY)
    fz_r = fresh_index(1, NZ)
    oy_r = fresh_index(1, NY)
    sy_r = fresh_index(1, NY)
    oz_r = fresh_index(1, NZ)
    sz_r = fresh_index(1, NZ)
    b_r = fresh_index(1, NR)

    pl.semaphore_wait(barrier, len(peers))

    for o in range(1, NR):
        push(xsend.at[o], xrecv.at[me], x_r + o, xpeer[o])
    for o in zorder:
        push(qo.at[t], qo.at[t], qoz_r + o, zpeer[o])
    for o in range(1, NY):
        push(qo.at[t], qo.at[t], qoy_r + o, ypeer[o])

    w_copy.wait()
    hidden = jnp.concatenate(
        [h_ref[0].astype(F32), jnp.zeros((1, 512), F32), h_ref[1].astype(F32), jnp.zeros((1, 512), F32)], axis=0
    ).astype(BF16)
    for kind in range(2):
        for k in range(0, KVH, 2):
            first = (kind * KVH + k) * HD
            part = jnp.dot(hidden, w[:, first:first + 2 * HD], preferred_element_type=F32)
            fsend[k // 2, 0, kind] = part[:, :HD]
            fsend[k // 2, 1, kind] = part[:, HD:]

    def forward(buf, chunk_r, out_r, offsets):
        for o in offsets:
            at = y * NZ + (z - o) % NZ
            arrive(buf.at[at], chunk_r + o)
            for yo in range(1, NY):
                push(buf.at[at], buf.at[at], out_r + yo, ypeer[yo])

    forward(qo, qoz_r, qoy_r, (1, 7))
    for o in range(1, NR):
        arrive(xrecv.at[(me - o) % NR], x_r + o)
    qs[t] = xrecv[...].reshape(NR * 8, HD).astype(BF16)
    for o in zorder:
        push(qs.at[t], qs.at[t], qsz_r + o, zpeer[o])
    forward(qo, qoz_r, qoy_r, (2, 6, 3, 5, 4))
    for yo in range(1, NY):
        push(qs.at[t], qs.at[t], qsy_r + yo, ypeer[yo])

    row_id = lax.broadcasted_iota(jnp.int32, (HD, HD), 0)
    both = jnp.bitwise_and(row_id, lanes((HD, HD)))
    parity = jnp.zeros((HD, HD), jnp.int32)
    for bit in range(7):
        parity = parity + jnp.bitwise_and(jnp.right_shift(both, bit), 1)
    signs = (1.0 - 2.0 * jnp.bitwise_and(parity, 1).astype(F32)).astype(BF16)

    pool_copy.wait()

    def round_trip(slot, carry):
        page = pool[slot]
        rows = jnp.concatenate([page[:, i * HD:(i + 1) * HD] for i in range(2 * KVH)], axis=0)
        turned = jnp.dot(rows, signs, preferred_element_type=F32) * INV
        scales = (jnp.max(jnp.abs(turned), axis=1, keepdims=True) + 1e-06).astype(BF16).astype(F32)
        packed = (turned * (1.0 / scales)).astype(BF16)
        back = (jnp.dot(packed, signs, preferred_element_type=F32) * (scales * INV)).astype(BF16)
        for i in range(2 * KVH):
            moved[slot, :, i * HD:(i + 1) * HD] = back[i * PAGE:(i + 1) * PAGE]
        return carry

    lax.fori_loop(0, SLOTS // 2, round_trip, 0)
    forward(qs, qsz_r, qsy_r, (1, 7, 2, 6, 3, 5, 4))
    for yo in range(1, NY):
        push(fsend.at[(y + yo) % NY], frecv.at[yo - 1], fy_r + yo, ypeer[yo])
    lax.fori_loop(SLOTS // 2, SLOTS, round_trip, 0)

    row16 = lax.broadcasted_iota(jnp.int32, (64, HD), 0) % 16
    lane64 = lanes((64, HD))
    first_half = row16 < 8
    mask_a = jnp.where(first_half, 1.0, 0.0).astype(BF16)
    mask_b = jnp.where(first_half, 0.0, 1.0).astype(BF16)
    place = ((lane64 // PAGE) * NT + t) * PAGE + lane64 % PAGE
    dest = lax.broadcasted_iota(jnp.int32, (64, HD), 0) // 16

    def attend(pages, queries, results, stats, pairs, describe, p):
        (slots_a, span_a), (slots_b, span_b) = describe(2 * p), describe(2 * p + 1)
        valid = place < jnp.where(first_half, span_a, span_b)
        at = pl.multiple_of(p * 16, 16)

        def tokens(slots, first):
            return jnp.concatenate([pages[slot, :, first:first + HD] for slot in slots], axis=0)

        for k in range(KVH):
            query = queries[4 * k:4 * k + 4, pl.ds(at, 16), :].reshape(64, HD)
            wide = jnp.concatenate([query * mask_a, query * mask_b], axis=1)
            keys = jnp.concatenate([tokens(slots_a, k * HD), tokens(slots_b, k * HD)], axis=1)
            score = lax.dot_general(wide, keys, (((1,), (1,)), ((), ())), preferred_element_type=F32) * INV
            score = jnp.where(valid, score, MASKED)
            top_high, top_mid = halves(jnp.max(score, axis=1, keepdims=True))
            weights = jnp.where(valid, jnp.exp(score - (top_high + top_mid)), 0.0)
            total_high, total_mid = halves(jnp.sum(weights, axis=1, keepdims=True))
            light = weights.astype(BF16)
            wide = jnp.concatenate([light * mask_a, light * mask_b], axis=1)
            values = jnp.concatenate(
                [tokens(slots_a, (KVH + k) * HD), tokens(slots_b, (KVH + k) * HD)], axis=0
            )
            mixed = jnp.dot(wide, values, preferred_element_type=F32).astype(BF16)
            for j in range(4):
                where = pl.multiple_of(((4 * (k % 2) + j) * pairs + p) * 16, 16)
                results[k // 2, pl.ds(where, 16), :] = mixed[j * 16:(j + 1) * 16]
            lane = lane64 - (4 * (k % 2) + dest) * (4 * pairs) - p
            tile = jnp.where(lane == 0, top_high, 0.0)
            tile = jnp.where(lane == pairs, top_mid, tile)
            tile = jnp.where(lane == 2 * pairs, total_high, tile)
            tile = jnp.where(lane == 3 * pairs, total_mid, tile)
            stats[k // 2] = stats[k // 2] + jnp.sum(tile.reshape(4, 16, HD), axis=0)

    def own(r):
        return [table[r, j] for j in range(PPD)], lengths[me, r]

    def taken(d):
        request = jnp.int32(0)
        for e in range(STEAL_IN):
            request = request + jnp.where(plan[d, e, 0] == me, plan[d, e, 1], 0)
        return [table[request, j] for j in range(PPD)], lengths[me, request]

    def own_pair(p, carry):
        attend(pool, qo, obo, sto, NPO, own, p)
        return carry

    def taken_pair(p, carry):
        attend(moved, qs, obs, sts, NPS, taken, p)
        return carry

    for yo in range(1, NY):
        first = ((y - yo) % NY) * NZ
        arrive(qo.at[pl.ds(first, NZ)], qoy_r + yo)
    lax.fori_loop(0, NPO, own_pair, 0)
    for c in range(NY):
        obo[c, NZ * NPO * 16:(NZ * NPO + 1) * 16, :] = sto[c].astype(BF16)
    for yo in range(1, NY):
        push(obo.at[(y + yo) % NY], rbo.at[yo - 1], oy_r + yo, ypeer[yo])

    for yo in range(1, NY):
        arrive(frecv.at[yo - 1], fy_r + yo)
    for c in range(2):
        for kind in range(2):
            fsum[c, kind] = fsend[y, c, kind] + frecv[0, c, kind] + frecv[1, c, kind] + frecv[2, c, kind]
    for o in zorder:
        push(fsum.at[((z + o) % NZ) // 4], fz.at[o - 1], fz_r + o, zpeer[o])

    for yo in range(1, NY):
        first = ((y - yo) % NY) * NZ
        arrive(qs.at[pl.ds(first, NZ)], qsy_r + yo)
    lax.fori_loop(0, NPS, taken_pair, 0)
    for c in range(NY):
        obs[c, NZ * NPS * 16:(NZ * NPS + 1) * 16, :] = sts[c].astype(BF16)
    for yo in range(1, NY):
        push(obs.at[(y + yo) % NY], rbs.at[yo - 1], sy_r + yo, ypeer[yo])

    lane16 = lanes((16, HD))

    def merge_y(mine, others, out, pairs):
        at = NZ * pairs * 16
        tiles = [mine[y, at:at + 16, :].astype(F32)]
        tiles += [others[i, at:at + 16, :].astype(F32) for i in range(NY - 1)]
        top, total, factors = merged_stats(tiles, pairs)
        top_high, top_mid = halves(top)
        total_high, total_mid = halves(total)
        phase = lane16 % (4 * pairs)
        stat = jnp.where(
            phase < pairs, top_high,
            jnp.where(
                phase < 2 * pairs, rolled(top_mid, pairs),
                jnp.where(phase < 3 * pairs, rolled(total_high, 2 * pairs), rolled(total_mid, 3 * pairs)),
            ),
        ).astype(BF16)
        for c in range(NZ):
            for p in range(pairs):
                lane = c * 4 * pairs + p
                rows = slice((c * pairs + p) * 16, (c * pairs + p + 1) * 16)
                acc = factors[0][:, lane:lane + 1] * mine[y, rows, :].astype(F32)
                for i in range(NY - 1):
                    acc = acc + factors[i + 1][:, lane:lane + 1] * others[i, rows, :].astype(F32)
                out[c, p * 16:(p + 1) * 16, :] = acc.astype(BF16)
            out[c, pairs * 16:(pairs + 1) * 16, :] = stat

    def merge_z(mine, others, pairs):
        at = pairs * 16
        shift = (128 - z * (4 * pairs)) % 128
        tiles = [mine[z, at:at + 16, :].astype(F32)]
        tiles += [others[i, at:at + 16, :].astype(F32) for i in range(NZ - 1)]
        top, total, factors = merged_stats([pltpu.roll(tile, shift, 1) for tile in tiles], pairs)
        result = []
        for p in range(pairs):
            rows = slice(p * 16, (p + 1) * 16)
            acc = factors[0][:, p:p + 1] * mine[z, rows, :].astype(F32)
            for i in range(NZ - 1):
                acc = acc + factors[i + 1][:, p:p + 1] * others[i, rows, :].astype(F32)
            result.append((acc, top[:, p:p + 1], total[:, p:p + 1]))
        return result

    for yo in range(1, NY):
        arrive(rbo.at[yo - 1], oy_r + yo)
    merge_y(obo, rbo, mbo, NPO)
    for o in zorder:
        push(mbo.at[(z + o) % NZ], zbo.at[o - 1], oz_r + o, zpeer[o])
    for yo in range(1, NY):
        arrive(rbs.at[yo - 1], sy_r + yo)
    merge_y(obs, rbs, mbs, NPS)
    for o in zorder:
        push(mbs.at[(z + o) % NZ], zbs.at[o - 1], sz_r + o, zpeer[o])

    for o in range(1, NZ):
        arrive(fz.at[o - 1], fz_r + o)
    for kind in range(2):
        acc = fsum[z // 4, kind]
        for o in range(1, NZ):
            acc = acc + fz[o - 1, kind]
        fresh[kind] = acc.astype(BF16).astype(F32)

    late = lax.broadcasted_iota(jnp.int32, (8, 1), 0) >= 4

    def finish(r, acc, top, total):
        query = qt[r * 8:(r + 1) * 8]
        tail = [jnp.sum(query * fresh[0, s * 8 + r:s * 8 + r + 1, :], axis=1, keepdims=True) * INV for s in range(2)]
        tail[1] = jnp.where(late, tail[1], MASKED)
        peak = jnp.maximum(top, jnp.maximum(tail[0], tail[1]))
        factor = jnp.exp(top - peak)
        first = jnp.exp(tail[0] - peak)
        second = jnp.where(late, jnp.exp(tail[1] - peak), 0.0)
        total = total * factor + first + second
        acc = acc * factor
        acc = acc + first.astype(BF16).astype(F32) * fresh[1, r:r + 1, :]
        acc = acc + second.astype(BF16).astype(F32) * fresh[1, 8 + r:8 + r + 1, :]
        fin[r * 8:(r + 1) * 8] = acc / total

    for o in range(1, NZ):
        arrive(zbo.at[o - 1], oz_r + o)
    for p, (acc, top, total) in enumerate(merge_z(mbo, zbo, NPO)):
        for i in range(2):
            rows = slice(i * 8, (i + 1) * 8)
            finish(2 * p + i, acc[rows], top[rows], total[rows])

    for o in range(1, NZ):
        arrive(zbs.at[o - 1], sz_r + o)
    lane8 = lanes((8, HD))
    for p, (acc, top, total) in enumerate(merge_z(mbs, zbs, NPS)):
        for i in range(2):
            rows = slice(i * 8, (i + 1) * 8)
            bsend[2 * p + i, 0:8] = acc[rows]
            bsend[2 * p + i, 8:16] = jnp.where(lane8 < 64, top[rows], total[rows])
    for o in range(1, NR):
        push(bsend.at[(me + o) % NR], brecv.at[me], b_r + o, xpeer[o])
    for o in range(1, NR):
        arrive(brecv.at[(me - o) % NR], b_r + o)
    for e in range(STEAL_IN):
        source = plan[me, e, 0]
        tile = brecv[source]
        finish(ROWS + e, tile[0:8], tile[8:16, 0:1], tile[8:16, 64:65])

    for s in range(2):
        for j in range(4):
            out_ref[s, :, j * HD:(j + 1) * HD] = fin[pl.ds(s * 4 + j, ROWS_ALL, stride=8), :].astype(BF16)

    for copy in sends:
        copy.wait_send()


def on_device(kv_pool, page_table, lengths, steal_plan, hidden_rows, kv_weight, queries):
    smem = pl.BlockSpec(memory_space=pltpu.SMEM)
    vmem = pl.BlockSpec(memory_space=pltpu.VMEM)
    hbm = pl.BlockSpec(memory_space=pl.ANY)
    width = 2 * KVH * HD
    tall = lambda n, *lead: pltpu.VMEM((*lead, n, HD), BF16)
    full = lambda n, *lead: pltpu.VMEM((*lead, n, HD), F32)
    out = pl.pallas_call(
        kernel,
        out_shape=jax.ShapeDtypeStruct((2, ROWS_ALL, 512), BF16),
        in_specs=[smem, smem, smem, vmem, vmem, hbm, hbm],
        out_specs=vmem,
        scratch_shapes=[
            pltpu.VMEM((SLOTS, PAGE, width), BF16),
            pltpu.VMEM((SLOTS, PAGE, width), BF16),
            pltpu.VMEM((512, width), BF16),
            full(ROWS_ALL * 8),
            tall(32, NT), tall(64, NT),
            full(8, NR), full(8, NR),
            full(16, NY, 2, 2), full(16, NY - 1, 2, 2), full(16, 2, 2), full(16, NZ - 1, 2), full(16, 2),
            tall((NZ * NPO + 1) * 16, NY), tall((NZ * NPS + 1) * 16, NY),
            tall((NZ * NPO + 1) * 16, NY - 1), tall((NZ * NPS + 1) * 16, NY - 1),
            full(16, NY), full(16, NY),
            tall((NPO + 1) * 16, NZ), tall((NPS + 1) * 16, NZ),
            tall((NPO + 1) * 16, NZ - 1), tall((NPS + 1) * 16, NZ - 1),
            full(16, NR), full(16, NR),
            full(ROWS_ALL * 8),
            pltpu.SemaphoreType.DMA((2,)),
            pltpu.SemaphoreType.DMA((128,)),
            pltpu.SemaphoreType.DMA((96,)),
        ],
        compiler_params=pltpu.CompilerParams(
            collective_id=0, has_side_effects=True, vmem_limit_bytes=48 * 2**20
        ),
    )(page_table[0], lengths, steal_plan, queries[0], hidden_rows[0], kv_pool[0], kv_weight)
    return out[None]


def solution(mesh):
    return jax.shard_map(
        on_device,
        mesh=mesh,
        in_specs=(
            P("replica", "tensor", None, None),
            P("replica", None, "tensor"),
            P(),
            P(),
            P("replica", None, None, "tensor"),
            P("tensor", None),
            P("replica", None, None, "tensor"),
        ),
        out_specs=P("replica", None, None, "tensor"),
        check_vma=False,
    )
```

time: 596 us -> 64.9 us (0.11)
  blocking collectives: 235 us -> 0 us
  waiting for transfers between devices: 174 us -> 0 us
  other arithmetic: 98.7 us -> 0 us
  Pallas kernels: 0 us -> 57.9 us
  local copies, waits for them, and re-layouts: 41.4 us -> 6.74 us
  matrix products: 17.7 us -> 0 us
  between operations: 13.7 us -> 0.01 us
  starting transfers between devices: 11.4 us -> 0 us
    all_gather x1 -> x0, waiting for transfers between devices: 174 us -> none  [joined(): everything = jax.tree.map(lambda part: lax.all_gather(part, axis), array)]
    psum x1 -> x0, blocking collectives: 118 us -> none  [on_device(): fresh = lax.psum(partial_value.astype(jnp.bfloat16), 'tensor')]
    all_gather x3 -> x0, blocking collectives: 117 us -> none  [the longest x2 81.4 us: joined(): everything = jax.tree.map(lambda part: lax.all_gather(part, axis), array)]
    add x65 -> x0, other arithmetic: 84 us -> none  [the longest x31 55.6 us: combine_partials(): first[2] * first_factor[..., None] + second[2] * second_factor[..., None]]
    pallas_call x0 -> x1, Pallas kernels: none -> 57.9 us  [on_device(): pl.pallas_call(kernel, out_shape=jax.ShapeDtypeStruct((2, ROWS_ALL, 512),...]
    dot_general x7 -> x0, matrix products: 17.7 us -> none  [the longest x1 5.82 us: rotate_pack(): jnp.einsum('...d,de->...e', shaped, rotation, precision=lax.Precision.HIG...]
    all_to_all x2 -> x0, starting transfers between devices: 11.4 us -> none  [the longest x1 6.46 us: on_device(): lax.all_to_all(scales, 'replica', split_axis=0, concat_axis=0, tiled=True)]
    gather x6 -> x0, local copies, waits for them, and re-layouts: 11.3 us -> none  [the longest x1 4.04 us: on_device(): jnp.take(arrived, landing, axis=0)]
  transfers between devices with their start and end apart: 3 -> 0, of which waited for: 1 -> 0; matrix products, arithmetic and copies ran while one was open for 4% -> 0% of each run, Pallas kernels for 0% -> 0%
where the time goes in v1:
time: 64.9 us; the launch traced here: 64.6 us
  Pallas kernels  57.9 us (89%)
  local copies, waits for them, and re-layouts  6.74 us (10%)
    pallas_call x1, Pallas kernels, on_device(): pl.pallas_call(kernel, out_shape=jax.ShapeDtypeStruct((2, ROWS_ALL, 512),...  57.9 us
    unnamed x8, local copies, waits for them, and re-layouts  5.39 us

profile of v1, /device:TPU:1, one launch (start us, length us, event | category | flops | bytes accessed | tf_op | source)
XLA Modules:
  0.0 64.6 jit_solution(8029590579841688100)
XLA Ops:
  0.0 0.8 %copy.10.lengths = s32[8,4]{1,0:T(8,128)S(1)} copy(s32[8,4]{0,1:T(4,128)} %param.9) | data formatting | bytes 256 | tf_op args[2]
  0.8 0.8 %copy.11.plan = s32[8,3,2]{2,1,0:T(4,128)S(1)} copy(s32[8,3,2]{0,2,1:T(2,128)} %param.10) | data formatting | bytes 384 | tf_op args[3]
  1.5 0.7 %copy_bitcast_fusion = (bf16[2,7,512]{2,1,0:T(8,128)(2,1)S(1)}, bf16[2,7,512]{2,1,0:T(8,128)(2,1)S(1)}) fusion(bf16[1,2,7,512]{3,1,2,0:T(2,128)(2,1)} %param.11, bf16[1,2,7,512]{3,1,2,0:T(2,128)(2,1)} %param.13), kind=kLoop, calls=%fused_computation | loop fusion | bytes 57344 | tf_op jit(solution)/shard_map/squeeze | solution.py:421
  2.3 0.0 copy-start
  2.3 1.6 %copy-done = bf16[1,16,32,2048]{3,2,1,0:T(8,128)(2,1)S(1)} copy-done((bf16[1,16,32,2048]{3,2,1,0:T(8,128)(2,1)S(1)}, bf16[1,16,32,2048]{3,2,1,0:T(8,128)(2,1)}, u32[]{:S(2)}) %copy-start) | copy-done | bytes 2097176
  3.9 0.0 copy-start.1
  3.9 1.6 %copy-done.1 = bf16[512,2048]{1,0:T(8,128)(2,1)S(1)} copy-done((bf16[512,2048]{1,0:T(8,128)(2,1)S(1)}, bf16[512,2048]{1,0:T(8,128)(2,1)}, u32[]{:S(2)}) %copy-start.1) | copy-done | bytes 2097176
  5.5 0.0 copy-start.2
  5.5 0.7 %copy-done.2 = s32[1,4,4]{2,1,0:T(4,128)S(1)} copy-done((s32[1,4,4]{2,1,0:T(4,128)S(1)}, s32[1,4,4]{2,1,0:T(4,128)}, u32[]{:S(2)}) %copy-start.2) | copy-done | bytes 88
  6.1 57.9 %shard_map.73 = bf16[2,7,512]{2,1,0:T(8,128)(2,1)S(1)} custom-call(s32[4,4]{1,0:T(4,128)S(1)} %bitcast.9, s32[8,4]{1,0:T(8,128)S(1)} %copy.10.lengths, s32[8,3,2]{2,1,0:T(4,128)S(1)} %copy.11.plan, bf16[2,7,512]{2,1,0:T(8,128)(2,1)S(1)} %get-tuple-element.6.q_ref, bf16[2,7,512]{2,1,0:T(8,128)(2,1)S(1)} %get-tuple-element.5.h_ref, ...), custom_call_target="tpu_custom_call" | custom-call | tf_op jit(solution)/shard_map/pallas_call | solution.py:394
  64.0 0.6 copy.12
Async XLA Ops:
  2.3 1.6 %copy-start = (bf16[1,16,32,2048]{3,2,1,0:T(8,128)(2,1)S(1)}, bf16[1,16,32,2048]{3,2,1,0:T(8,128)(2,1)}, u32[]{:S(2)}) copy-start(bf16[1,16,32,2048]{3,2,1,0:T(8,128)(2,1)} %param.7) | copy-start | bytes 6291460
  3.9 1.6 %copy-start.1 = (bf16[512,2048]{1,0:T(8,128)(2,1)S(1)}, bf16[512,2048]{1,0:T(8,128)(2,1)}, u32[]{:S(2)}) copy-start(bf16[512,2048]{1,0:T(8,128)(2,1)} %w_hbm.1) | copy-start | bytes 6291460
  5.5 0.7 %copy-start.2 = (s32[1,4,4]{2,1,0:T(4,128)S(1)}, s32[1,4,4]{2,1,0:T(4,128)}, u32[]{:S(2)}) copy-start(s32[1,4,4]{2,1,0:T(4,128)} %param.8) | copy-start | bytes 196

commit v2 on v1

--- a/solution.py
+++ b/solution.py
@@ -55,8 +55,8 @@
 
 
 def kernel(
-    table, lengths, plan, q_ref, h_ref, pool_hbm, w_hbm, out_ref,
-    pool, moved, w, qt, qo, qs, xsend, xrecv, fsend, frecv, fsum, fz, fresh,
+    table_hbm, lengths_hbm, plan_hbm, q_hbm, h_hbm, pool_hbm, w_hbm, out_ref,
+    table, lengths, plan, q_ref, h_ref, pool, moved, w, qt, qo, qs, xsend, xrecv, fsend, frecv, fsum, fz, fresh,
     obo, obs, rbo, rbs, sto, sts, mbo, mbs, zbo, zbs, bsend, brecv, fin,
     lsem, ss, rs,
 ):
@@ -68,26 +68,29 @@
     xpeer = [None] + [((me + o) % NR, t) for o in range(1, NR)]
     zorder = (1, 7, 2, 6, 3, 5, 4)
 
-    pool_copy = pltpu.make_async_copy(pool_hbm, pool, lsem.at[0])
-    w_copy = pltpu.make_async_copy(w_hbm, w, lsem.at[1])
-    w_copy.start()
-    pool_copy.start()
+    pairs = ((q_hbm, q_ref), (plan_hbm, plan), (h_hbm, h_ref), (w_hbm, w), (pool_hbm, pool), (table_hbm, table), (lengths_hbm, lengths))
+    copies = [pltpu.make_async_copy(src, dst, lsem.at[i]) for i, (src, dst) in enumerate(pairs)]
+    q_copy, plan_copy, h_copy, w_copy, pool_copy, table_copy, lengths_copy = copies
+    for copy in copies:
+        copy.start()
 
     barrier = pltpu.get_barrier_semaphore()
     peers = zpeer[1:] + ypeer[1:] + xpeer[1:]
     for peer in peers:
         pl.semaphore_signal(barrier, inc=1, device_id=peer, device_id_type=MESH)
 
+    q_copy.wait()
+    plan_copy.wait()
     for s in range(2):
         for j in range(4):
-            qt[pl.ds(s * 4 + j, ROWS_ALL, stride=8), :] = q_ref[s, :, j * HD:(j + 1) * HD].astype(F32)
+            qt[pl.ds(s * 4 + j, ROWS_ALL, stride=8), :] = q_ref[:, s, j * HD:(j + 1) * HD].astype(F32)
     qo[t] = qt[0:32].astype(BF16)
     for o in range(1, NR):
         source = (me + o) % NR
         chosen = jnp.zeros((8, HD), F32)
         for e in range(STEAL_IN):
             tile = qt[(ROWS + e) * 8:(ROWS + e + 1) * 8]
-            chosen = chosen + jnp.where(plan[me, e, 0] == source, tile, 0.0)
+            chosen = chosen + jnp.where(plan[e, 0, me] == source, tile, 0.0)
         xsend[o] = chosen
     xrecv[me] = jnp.zeros((8, HD), F32)
     sto[...] = jnp.zeros_like(sto)
@@ -138,8 +141,9 @@
         push(qo.at[t], qo.at[t], qoy_r + o, ypeer[o])
 
     w_copy.wait()
+    h_copy.wait()
     hidden = jnp.concatenate(
-        [h_ref[0].astype(F32), jnp.zeros((1, 512), F32), h_ref[1].astype(F32), jnp.zeros((1, 512), F32)], axis=0
+        [h_ref[:, 0].astype(F32), jnp.zeros((1, 512), F32), h_ref[:, 1].astype(F32), jnp.zeros((1, 512), F32)], axis=0
     ).astype(BF16)
     for kind in range(2):
         for k in range(0, KVH, 2):
@@ -173,6 +177,8 @@
     signs = (1.0 - 2.0 * jnp.bitwise_and(parity, 1).astype(F32)).astype(BF16)
 
     pool_copy.wait()
+    table_copy.wait()
+    lengths_copy.wait()
 
     def round_trip(slot, carry):
         page = pool[slot]
@@ -185,11 +191,11 @@
             moved[slot, :, i * HD:(i + 1) * HD] = back[i * PAGE:(i + 1) * PAGE]
         return carry
 
-    lax.fori_loop(0, SLOTS // 2, round_trip, 0)
+    lax.fori_loop(0, SLOTS // 2, round_trip, 0, unroll=4)
     forward(qs, qsz_r, qsy_r, (1, 7, 2, 6, 3, 5, 4))
     for yo in range(1, NY):
         push(fsend.at[(y + yo) % NY], frecv.at[yo - 1], fy_r + yo, ypeer[yo])
-    lax.fori_loop(SLOTS // 2, SLOTS, round_trip, 0)
+    lax.fori_loop(SLOTS // 2, SLOTS, round_trip, 0, unroll=4)
 
     row16 = lax.broadcasted_iota(jnp.int32, (64, HD), 0) % 16
     lane64 = lanes((64, HD))
@@ -207,39 +213,48 @@
         def tokens(slots, first):
             return jnp.concatenate([pages[slot, :, first:first + HD] for slot in slots], axis=0)
 
+        scores, tops, lights, totals, mixed = [], [], [], [], []
         for k in range(KVH):
             query = queries[4 * k:4 * k + 4, pl.ds(at, 16), :].reshape(64, HD)
             wide = jnp.concatenate([query * mask_a, query * mask_b], axis=1)
             keys = jnp.concatenate([tokens(slots_a, k * HD), tokens(slots_b, k * HD)], axis=1)
-            score = lax.dot_general(wide, keys, (((1,), (1,)), ((), ())), preferred_element_type=F32) * INV
-            score = jnp.where(valid, score, MASKED)
-            top_high, top_mid = halves(jnp.max(score, axis=1, keepdims=True))
-            weights = jnp.where(valid, jnp.exp(score - (top_high + top_mid)), 0.0)
-            total_high, total_mid = halves(jnp.sum(weights, axis=1, keepdims=True))
-            light = weights.astype(BF16)
-            wide = jnp.concatenate([light * mask_a, light * mask_b], axis=1)
+            scores.append(lax.dot_general(wide, keys, (((1,), (1,)), ((), ())), preferred_element_type=F32))
+        for k in range(KVH):
+            scores[k] = jnp.where(valid, scores[k] * INV, MASKED)
+            tops.append(halves(jnp.max(scores[k], axis=1, keepdims=True)))
+        for k in range(KVH):
+            weights = jnp.where(valid, jnp.exp(scores[k] - (tops[k][0] + tops[k][1])), 0.0)
+            totals.append(halves(jnp.sum(weights, axis=1, keepdims=True)))
+            lights.append(weights.astype(BF16))
+        for k in range(KVH):
+            wide = jnp.concatenate([lights[k] * mask_a, lights[k] * mask_b], axis=1)
             values = jnp.concatenate(
                 [tokens(slots_a, (KVH + k) * HD), tokens(slots_b, (KVH + k) * HD)], axis=0
             )
-            mixed = jnp.dot(wide, values, preferred_element_type=F32).astype(BF16)
+            mixed.append(jnp.dot(wide, values, preferred_element_type=F32).astype(BF16))
+        for k in range(KVH):
             for j in range(4):
                 where = pl.multiple_of(((4 * (k % 2) + j) * pairs + p) * 16, 16)
-                results[k // 2, pl.ds(where, 16), :] = mixed[j * 16:(j + 1) * 16]
-            lane = lane64 - (4 * (k % 2) + dest) * (4 * pairs) - p
-            tile = jnp.where(lane == 0, top_high, 0.0)
-            tile = jnp.where(lane == pairs, top_mid, tile)
-            tile = jnp.where(lane == 2 * pairs, total_high, tile)
-            tile = jnp.where(lane == 3 * pairs, total_mid, tile)
-            stats[k // 2] = stats[k // 2] + jnp.sum(tile.reshape(4, 16, HD), axis=0)
+                results[k // 2, pl.ds(where, 16), :] = mixed[k][j * 16:(j + 1) * 16]
+        for c in range(KVH // 2):
+            sums = stats[c]
+            for k in (2 * c, 2 * c + 1):
+                lane = lane64 - (4 * (k % 2) + dest) * (4 * pairs) - p
+                tile = jnp.where(lane == 0, tops[k][0], 0.0)
+                tile = jnp.where(lane == pairs, tops[k][1], tile)
+                tile = jnp.where(lane == 2 * pairs, totals[k][0], tile)
+                tile = jnp.where(lane == 3 * pairs, totals[k][1], tile)
+                sums = sums + jnp.sum(tile.reshape(4, 16, HD), axis=0)
+            stats[c] = sums
 
     def own(r):
-        return [table[r, j] for j in range(PPD)], lengths[me, r]
+        return [table[r, j] for j in range(PPD)], lengths[r, me]
 
     def taken(d):
         request = jnp.int32(0)
         for e in range(STEAL_IN):
-            request = request + jnp.where(plan[d, e, 0] == me, plan[d, e, 1], 0)
-        return [table[request, j] for j in range(PPD)], lengths[me, request]
+            request = request + jnp.where(plan[e, 0, d] == me, plan[e, 1, d], 0)
+        return [table[request, j] for j in range(PPD)], lengths[request, me]
 
     def own_pair(p, carry):
         attend(pool, qo, obo, sto, NPO, own, p)
@@ -372,31 +387,35 @@
     for o in range(1, NR):
         arrive(brecv.at[(me - o) % NR], b_r + o)
     for e in range(STEAL_IN):
-        source = plan[me, e, 0]
+        source = plan[e, 0, me]
         tile = brecv[source]
         finish(ROWS + e, tile[0:8], tile[8:16, 0:1], tile[8:16, 64:65])
 
     for s in range(2):
         for j in range(4):
-            out_ref[s, :, j * HD:(j + 1) * HD] = fin[pl.ds(s * 4 + j, ROWS_ALL, stride=8), :].astype(BF16)
+            out_ref[:, s, j * HD:(j + 1) * HD] = fin[pl.ds(s * 4 + j, ROWS_ALL, stride=8), :].astype(BF16)
 
     for copy in sends:
         copy.wait_send()
 
 
 def on_device(kv_pool, page_table, lengths, steal_plan, hidden_rows, kv_weight, queries):
-    smem = pl.BlockSpec(memory_space=pltpu.SMEM)
     vmem = pl.BlockSpec(memory_space=pltpu.VMEM)
-    hbm = pl.BlockSpec(memory_space=pl.ANY)
+    hbm = pl.BlockSpec(memory_space=pltpu.HBM)
     width = 2 * KVH * HD
     tall = lambda n, *lead: pltpu.VMEM((*lead, n, HD), BF16)
     full = lambda n, *lead: pltpu.VMEM((*lead, n, HD), F32)
     out = pl.pallas_call(
         kernel,
-        out_shape=jax.ShapeDtypeStruct((2, ROWS_ALL, 512), BF16),
-        in_specs=[smem, smem, smem, vmem, vmem, hbm, hbm],
+        out_shape=jax.ShapeDtypeStruct((ROWS_ALL, 2, 512), BF16),
+        in_specs=[hbm] * 7,
         out_specs=vmem,
         scratch_shapes=[
+            pltpu.SMEM((ROWS, PPD), jnp.int32),
+            pltpu.SMEM((ROWS, NR), jnp.int32),
+            pltpu.SMEM((STEAL_IN, 2, NR), jnp.int32),
+            pltpu.VMEM((ROWS_ALL, 2, 512), BF16),
+            pltpu.VMEM((ROWS_ALL, 2, 512), BF16),
             pltpu.VMEM((SLOTS, PAGE, width), BF16),
             pltpu.VMEM((SLOTS, PAGE, width), BF16),
             pltpu.VMEM((512, width), BF16),
@@ -411,15 +430,18 @@
             tall((NPO + 1) * 16, NZ - 1), tall((NPS + 1) * 16, NZ - 1),
             full(16, NR), full(16, NR),
             full(ROWS_ALL * 8),
-            pltpu.SemaphoreType.DMA((2,)),
+            pltpu.SemaphoreType.DMA((7,)),
             pltpu.SemaphoreType.DMA((128,)),
             pltpu.SemaphoreType.DMA((96,)),
         ],
         compiler_params=pltpu.CompilerParams(
-            collective_id=0, has_side_effects=True, vmem_limit_bytes=48 * 2**20
+            collective_id=0, has_side_effects=True, vmem_limit_bytes=63 * 2**20
         ),
-    )(page_table[0], lengths, steal_plan, queries[0], hidden_rows[0], kv_pool[0], kv_weight)
-    return out[None]
+    )(
+        page_table[0], lengths.T, steal_plan.transpose(1, 2, 0), queries[0].transpose(1, 0, 2),
+        hidden_rows[0].transpose(1, 0, 2), kv_pool[0], kv_weight,
+    )
+    return out.transpose(1, 0, 2)[None]
 
 
 def solution(mesh):

time: 64.9 us -> 50.3 us (0.78)
  Pallas kernels: 57.9 us -> 48.7 us
  local copies, waits for them, and re-layouts: 6.74 us -> 1.32 us
    pallas_call x1, Pallas kernels: 57.9 us -> 48.7 us  [on_device(): pl.pallas_call(kernel, out_shape=jax.ShapeDtypeStruct((ROWS_ALL, 2, 512),...]
    unnamed x8 -> x1, local copies, waits for them, and re-layouts: 5.39 us -> 1.32 us
    squeeze x1 -> x0, local copies, waits for them, and re-layouts: 0.74 us -> none  [on_device(): hidden_rows[0]]
where the time goes in v2:
time: 50.3 us; the launch traced here: 50 us
  Pallas kernels  48.7 us (97%)
  local copies, waits for them, and re-layouts  1.32 us (3%)
    pallas_call x1, Pallas kernels, on_device(): pl.pallas_call(kernel, out_shape=jax.ShapeDtypeStruct((ROWS_ALL, 2, 512),...  48.7 us
    unnamed x1, local copies, waits for them, and re-layouts  1.32 us

profile of v2, /device:TPU:1, one launch (start us, length us, event | category | flops | bytes accessed | tf_op | source)
XLA Modules:
  0.0 50.0 jit_solution(528469765183027220)
XLA Ops:
  0.0 48.7 %shard_map.73 = bf16[7,2,512]{2,1,0:T(2,128)(2,1)} custom-call(s32[4,4]{1,0:T(4,128)} %bitcast.18, s32[4,8]{1,0:T(4,128)} %bitcast.19, s32[3,2,8]{2,1,0:T(2,128)} %bitcast.17, bf16[7,2,512]{2,1,0:T(2,128)(2,1)} %bitcast.15, bf16[7,2,512]{2,1,0:T(2,128)(2,1)} %bitcast.16, bf16[16,32,2048]{2,1,0:T(8,128)(2,1)} %bitcast.13, bf16[512,2048]{1,0:T(8,128)(2,1)} %w_hbm.1), custom_call_target="tpu_custom_call" | custom-call | tf_op jit(solution)/shard_map/pallas_call | solution.py:408
  48.7 1.3 %copy.9 = bf16[1,2,7,512]{3,1,2,0:T(2,128)(2,1)} copy(bf16[1,2,7,512]{3,1,2,0:T(2,128)(2,1)} %bitcast.14) | data formatting | bytes 28672

commit v3 on v2

v3 whole, which is shorter than its diff:
```python
import functools
import math

import jax
import jax.numpy as jnp
from jax import lax
from jax.experimental import pallas as pl
from jax.experimental.pallas import tpu as pltpu
from jax.sharding import PartitionSpec as P

KVH = 8
HD = 128
PAGE = 32
PPD = 4
STEAL_IN = 3
ROWS = 4
ROWS_ALL = 7
SLOTS = 16
NR = 8
NY = 4
NZ = 8
NT = NY * NZ
MASKED = -1e30
MESH = pl.DeviceIdType.MESH
F32 = jnp.float32
BF16 = jnp.bfloat16
INV = 1.0 / math.sqrt(HD)
OWN = ROWS * 64 + 16
ONE = 64 + 16


def lanes(shape):
    return lax.broadcasted_iota(jnp.int32, shape, len(shape) - 1)


def halves(x):
    high = x.astype(BF16).astype(F32)
    return high, (x - high).astype(BF16).astype(F32)


def stat_factors(tiles):
    tops = [tile + pltpu.roll(tile, 127, 1) for tile in tiles]
    totals = [pltpu.roll(one, 126, 1) for one in tops]
    top = functools.reduce(jnp.maximum, tops)
    factors = [jnp.exp(one - top) for one in tops]
    total = sum(f * l for f, l in zip(factors, totals))
    return top, total, factors


def column(x, first):
    return jnp.concatenate([x[:, first + 4 * g:first + 4 * g + 1] for g in range(4)], axis=0)


def merged(stat, first, parts):
    top, total, factors = stat
    acc = sum(column(f, first) * part.astype(F32) for f, part in zip(factors, parts))
    return acc, column(top, first), column(total, first)


def kernel(
    table_hbm, lengths_hbm, plan_hbm, q_hbm, h_hbm, pool_hbm, w_hbm, out_ref,
    table, lengths, plan, q_ref, h_ref, pool, moved, w, qt, qz, qown, qsend, qslot,
    fsend, frecv, fsum, fz, fresh, obo, rbo, obs, rbs, sto, macc, mst, mb, zb, fin,
    lsem, ss, rs, slot_rs,
):
    me = lax.axis_index("replica")
    t = lax.axis_index("tensor")
    y, z = t // NZ, t % NZ

    def near(o=0, yo=0, zo=0):
        return ((me + o) % NR, ((y + yo) % NY) * NZ + (z + zo) % NZ)

    zorder = (4, 3, 5, 2, 6, 1, 7)

    pairs = (
        (q_hbm, q_ref), (plan_hbm, plan), (h_hbm, h_ref), (w_hbm, w),
        (pool_hbm, pool), (table_hbm, table), (lengths_hbm, lengths),
    )
    copies = [pltpu.make_async_copy(src, dst, lsem.at[i]) for i, (src, dst) in enumerate(pairs)]
    q_copy, plan_copy, h_copy, w_copy, pool_copy, table_copy, lengths_copy = copies
    for copy in copies:
        copy.start()

    barrier = pltpu.get_barrier_semaphore()
    peers = [near(zo=o) for o in zorder] + [near(yo=o) for o in range(1, NY)]
    peers += [near(o, yo) for o in range(1, NR) for yo in range(NY)]
    for peer in peers:
        pl.semaphore_signal(barrier, inc=1, device_id=peer, device_id_type=MESH)

    q_copy.wait()
    for s in range(2):
        for j in range(4):
            qt[pl.ds(s * 4 + j, ROWS_ALL, stride=8), :] = q_ref[:, s, j * HD:(j + 1) * HD].astype(F32)
    qt[56:64] = jnp.zeros((8, HD), F32)
    qz[0] = qt[...].astype(BF16)
    qslot[NR - 1] = jnp.zeros((NY, 64, HD), BF16)
    sto[...] = jnp.zeros_like(sto)
    mst[...] = jnp.zeros_like(mst)

    def push(src, dst, stage, peer, recv=None):
        pltpu.make_async_remote_copy(
            src_ref=src, dst_ref=dst, send_sem=ss.at[stage], recv_sem=rs.at[stage] if recv is None else recv,
            device_id=peer, device_id_type=MESH,
        ).start()

    def whole(ref, stage, recv=None):
        return pltpu.make_async_remote_copy(
            src_ref=ref, dst_ref=ref, send_sem=ss.at[stage], recv_sem=rs.at[stage] if recv is None else recv,
            device_id=near(1), device_id_type=MESH,
        )

    QZ, QY, QX, FY, FZ, OY, OX, OZ = range(8)

    pl.semaphore_wait(barrier, len(peers))

    for o in zorder:
        push(qz.at[0], qz.at[o], QZ, near(zo=o))

    w_copy.wait()
    h_copy.wait()
    gap = jnp.zeros((1, 512), F32)
    hidden = jnp.concatenate([h_ref[:, 0].astype(F32), gap, h_ref[:, 1].astype(F32), gap], axis=0).astype(BF16)
    for kind in range(2):
        for k in range(0, KVH, 2):
            first = (kind * KVH + k) * HD
            part = jnp.dot(hidden, w[:, first:first + 2 * HD], preferred_element_type=F32)
            fsend[k // 2, 0, kind] = part[:, :HD]
            fsend[k // 2, 1, kind] = part[:, HD:]
    for yo in range(1, NY):
        push(fsend.at[(y + yo) % NY], frecv.at[yo - 1], FY, near(yo=yo))

    plan_copy.wait()
    whole(qz.at[1:NZ], QZ).wait_recv()
    chunks = [qz[(z - c + NZ) % NZ].astype(F32) for c in range(NZ)]

    def by_row(r):
        return jnp.concatenate([chunk[r * 8:(r + 1) * 8] for chunk in chunks], axis=0)

    for r in range(ROWS):
        qown[0, r] = by_row(r).astype(BF16)
    for yo in range(1, NY):
        push(qown.at[0], qown.at[yo], QY, near(yo=yo))
    leaving = [by_row(ROWS + e) for e in range(STEAL_IN)]
    for o in range(1, NR):
        source = (me - o + NR) % NR
        chosen = jnp.zeros((64, HD), F32)
        for e in range(STEAL_IN):
            chosen = chosen + jnp.where(plan[e, 0, me] == source, leaving[e], 0.0)
        qsend[o - 1] = chosen.astype(BF16)
        for yo in range(NY):
            push(qsend.at[o - 1], qslot.at[o - 1, yo], QX, near(-o + NR, yo), slot_rs.at[(o - 1) // 2])

    row_id = lax.broadcasted_iota(jnp.int32, (HD, HD), 0)
    both = jnp.bitwise_and(row_id, lanes((HD, HD)))
    parity = jnp.zeros((HD, HD), jnp.int32)
    for bit in range(7):
        parity = parity + jnp.bitwise_and(jnp.right_shift(both, bit), 1)
    signs = (1.0 - 2.0 * jnp.bitwise_and(parity, 1).astype(F32)).astype(BF16)

    pool_copy.wait()
    table_copy.wait()
    lengths_copy.wait()

    def round_trip(slot, carry):
        page = pool[slot]
        rows = jnp.concatenate([page[:, i * HD:(i + 1) * HD] for i in range(2 * KVH)], axis=0)
        turned = jnp.dot(rows, signs, preferred_element_type=F32) * INV
        scales = (jnp.max(jnp.abs(turned), axis=1, keepdims=True) + 1e-06).astype(BF16).astype(F32)
        packed = (turned * (1.0 / scales)).astype(BF16)
        back = (jnp.dot(packed, signs, preferred_element_type=F32) * (scales * INV)).astype(BF16)
        for i in range(2 * KVH):
            moved[slot, :, i * HD:(i + 1) * HD] = back[i * PAGE:(i + 1) * PAGE]
        return carry

    lax.fori_loop(0, SLOTS, round_trip, 0, unroll=4)

    lane64 = lanes((64, HD))
    row64 = lax.broadcasted_iota(jnp.int32, (64, HD), 0)
    upper = row64 < 32
    place = ((lane64 // PAGE) * NT + t) * PAGE + lane64 % PAGE
    blank = jnp.zeros((32, HD), BF16)

    def attend(pages, a, b, query, put, put_stats, lane_a, lane_b):
        (slots_a, span_a), (slots_b, span_b) = a, b
        valid = place < jnp.where(upper, span_a, span_b)

        def tokens(slots, first):
            return jnp.concatenate([pages[slot, :, first:first + HD] for slot in slots], axis=0)

        def spread(first, second):
            return jnp.concatenate(
                [jnp.concatenate([first, blank], axis=1), jnp.concatenate([blank, second], axis=1)], axis=0
            )

        scores, tops, lights, totals, mixed = [], [], [], [], []
        for k in range(KVH):
            wide = spread(query(0, k), query(1, k))
            keys = jnp.concatenate([tokens(slots_a, k * HD), tokens(slots_b, k * HD)], axis=1)
            scores.append(lax.dot_general(wide, keys, (((1,), (1,)), ((), ())), preferred_element_type=F32))
        for k in range(KVH):
            scores[k] = jnp.where(valid, scores[k] * INV, MASKED)
            tops.append(halves(jnp.max(scores[k], axis=1, keepdims=True)))
        for k in range(KVH):
            weights = jnp.where(valid, jnp.exp(scores[k] - (tops[k][0] + tops[k][1])), 0.0)
            totals.append(halves(jnp.sum(weights, axis=1, keepdims=True)))
            lights.append(weights.astype(BF16))
        for k in range(KVH):
            wide = spread(lights[k][:32], lights[k][32:])
            values = jnp.concatenate(
                [tokens(slots_a, (KVH + k) * HD), tokens(slots_b, (KVH + k) * HD)], axis=0
            )
            mixed.append(jnp.dot(wide, values, preferred_element_type=F32).astype(BF16))
        for k in range(KVH):
            put(0, k, mixed[k][:32])
            put(1, k, mixed[k][32:])
        shift = (row64 % 32) // 16 * 4 + jnp.where(upper, lane_a, lane_b)
        for c in range(KVH // 2):
            tile = jnp.zeros((64, HD), F32)
            for k in (2 * c, 2 * c + 1):
                lane = lane64 - shift - 8 * (k % 2)
                for i, piece in enumerate(tops[k] + totals[k]):
                    tile = jnp.where(lane == i, piece, tile)
            put_stats(0, c, tile[:16] + tile[16:32])
            put_stats(1, c, tile[32:48] + tile[48:])

    def pages_of(request):
        return [table[request, j] for j in range(PPD)], lengths[request, me]

    def own_pair(p, carry):
        def put(i, k, value):
            at = pl.multiple_of((2 * p + i) * 64 + (k % 2) * 32, 32)
            obo[k // 2, pl.ds(at, 32), :] = value

        def put_stats(i, c, tile):
            sto[c] = sto[c] + tile

        def query(i, k):
            return qown[(y - k // 2 + NY) % NY, 2 * p + i, (k % 2) * 32:(k % 2 + 1) * 32, :]

        attend(pool, pages_of(2 * p), pages_of(2 * p + 1), query, put, put_stats, 32 * p, 32 * p + 16)
        return carry

    def taken(o):
        taker = (me + o + 1) % NR
        request = jnp.int32(0)
        for e in range(STEAL_IN):
            request = request + jnp.where(plan[e, 0, taker] == me, plan[e, 1, taker], 0)
        return pages_of(request)

    def taken_pair(p, carry):
        def put(i, k, value):
            obs[2 * p + i, k // 2, (k % 2) * 32:(k % 2 + 1) * 32, :] = value

        def put_stats(i, c, tile):
            obs[2 * p + i, c, 64:80, :] = tile.astype(BF16)

        def query(i, k):
            return qslot[2 * p + i, (y - k // 2 + NY) % NY, (k % 2) * 32:(k % 2 + 1) * 32, :]

        attend(moved, taken(2 * p), taken(2 * p + 1), query, put, put_stats, 0, 0)
        return carry

    whole(qown.at[1:NY], QY).wait_recv()
    lax.fori_loop(0, ROWS // 2, own_pair, 0)
    for c in range(NY):
        obo[c, ROWS * 64:OWN, :] = sto[c].astype(BF16)
    for yo in range(1, NY):
        push(obo.at[(y + yo) % NY], rbo.at[yo - 1], OY, near(yo=yo))

    whole(frecv, FY).wait_recv()
    for c in range(2):
        for kind in range(2):
            fsum[c, kind] = fsend[y, c, kind] + frecv[0, c, kind] + frecv[1, c, kind] + frecv[2, c, kind]
    for o in zorder:
        push(fsum.at[((z + o) % NZ) // 4], fz.at[o - 1], FZ, near(zo=o))

    for p in range(NR // 2):
        whole(qslot.at[2 * p:min(2 * p + 2, NR - 1)], QX, slot_rs.at[p]).wait_recv()
        taken_pair(p, 0)
        for o in range(2 * p + 1, min(2 * p + 3, NR)):
            for yo in range(NY):
                push(obs.at[o - 1, (y + yo) % NY], rbs.at[o - 1, yo], OX, near(o, yo))

    def keep(r, acc, top, total):
        macc[r] = acc
        tile = jnp.zeros((64, HD), F32)
        for i, piece in enumerate(halves(top) + halves(total)):
            tile = jnp.where(lane64 == r // 2 * 4 + i, piece, tile)
        mst[r % 2] = mst[r % 2] + tile

    whole(rbo, OY).wait_recv()
    held = [obo.at[y]] + [rbo.at[i] for i in range(NY - 1)]
    stat = stat_factors([ref[ROWS * 64:OWN, :].astype(F32) for ref in held])
    for r in range(ROWS):
        keep(r, *merged(stat, 16 * r, [ref[r * 64:(r + 1) * 64, :] for ref in held]))

    whole(rbs, OX).wait_recv()
    for e in range(STEAL_IN):
        o = jnp.minimum((me - plan[e, 0, me] + 2 * NR - 1) % NR, NR - 2)
        parts = [rbs[o, i] for i in range(NY)]
        stat = stat_factors([part[64:].astype(F32) for part in parts])
        keep(ROWS + e, *merged(stat, 0, [part[:64] for part in parts]))

    for c in range(NZ):
        rows = slice(c * 8, (c + 1) * 8)
        mb[c, 0:64, :] = jnp.concatenate(
            [macc[r, rows, :] for r in range(ROWS_ALL)] + [jnp.zeros((8, HD), F32)], axis=0
        ).astype(BF16)
        mb[c, 64:80, :] = jnp.concatenate([mst[0, rows, :], mst[1, rows, :]], axis=0).astype(BF16)
    for o in zorder:
        push(mb.at[(z + o) % NZ], zb.at[o - 1], OZ, near(zo=o))

    whole(fz, FZ).wait_recv()
    for kind in range(2):
        acc = fsum[z // 4, kind]
        for o in range(1, NZ):
            acc = acc + fz[o - 1, kind]
        fresh[kind] = acc.astype(BF16).astype(F32)

    def new_rows(kind, s):
        return jnp.concatenate(
            [jnp.broadcast_to(fresh[kind, s * 8 + r:s * 8 + r + 1, :], (8, HD)) for r in range(8)], axis=0
        )

    late = lax.broadcasted_iota(jnp.int32, (64, 1), 0) % 8 >= 4
    query = qt[...]
    tail = [jnp.sum(query * new_rows(0, s), axis=1, keepdims=True) * INV for s in range(2)]
    tail[1] = jnp.where(late, tail[1], MASKED)
    tail_top = jnp.maximum(tail[0], tail[1])

    whole(zb, OZ).wait_recv()
    held = [mb.at[z]] + [zb.at[i] for i in range(NZ - 1)]
    stat = stat_factors([ref[64:ONE, :].astype(F32) for ref in held])
    acc, top, total = merged(stat, 0, [ref[0:64, :] for ref in held])
    peak = jnp.maximum(top, tail_top)
    factor = jnp.exp(top - peak)
    first = jnp.exp(tail[0] - peak)
    second = jnp.where(late, jnp.exp(tail[1] - peak), 0.0)
    total = total * factor + first + second
    acc = acc * factor
    acc = acc + first.astype(BF16).astype(F32) * new_rows(1, 0)
    acc = acc + second.astype(BF16).astype(F32) * new_rows(1, 1)
    fin[...] = acc / total
    for s in range(2):
        for j in range(4):
            out_ref[:, s, j * HD:(j + 1) * HD] = fin[pl.ds(s * 4 + j, ROWS_ALL, stride=8), :].astype(BF16)

    whole(qz.at[1:NZ], QZ).wait_send()
    whole(frecv, FY).wait_send()
    whole(qown.at[1:NY], QY).wait_send()
    whole(qslot.at[0:NR - 1], QX).wait_send()
    whole(rbo, OY).wait_send()
    whole(fz, FZ).wait_send()
    whole(rbs, OX).wait_send()
    whole(zb, OZ).wait_send()


def on_device(kv_pool, page_table, lengths, steal_plan, hidden_rows, kv_weight, queries):
    hbm = pl.BlockSpec(memory_space=pltpu.HBM)
    width = 2 * KVH * HD

    def half(*shape):
        return pltpu.VMEM((*shape, HD), BF16)

    def full(*shape):
        return pltpu.VMEM((*shape, HD), F32)

    out = pl.pallas_call(
        kernel,
        out_shape=jax.ShapeDtypeStruct((ROWS_ALL, 2, 512), BF16),
        in_specs=[hbm] * 7,
        out_specs=pl.BlockSpec(memory_space=pltpu.VMEM),
        scratch_shapes=[
            pltpu.SMEM((ROWS, PPD), jnp.int32),
            pltpu.SMEM((ROWS, NR), jnp.int32),
            pltpu.SMEM((STEAL_IN, 2, NR), jnp.int32),
            pltpu.VMEM((ROWS_ALL, 2, 512), BF16),
            pltpu.VMEM((ROWS_ALL, 2, 512), BF16),
            pltpu.VMEM((SLOTS, PAGE, width), BF16),
            pltpu.VMEM((SLOTS, PAGE, width), BF16),
            pltpu.VMEM((512, width), BF16),
            full(64), half(NZ, 64), half(NY, ROWS, 64), half(NR - 1, 64), half(NR, NY, 64),
            full(NY, 2, 2, 16), full(NY - 1, 2, 2, 16), full(2, 2, 16), full(NZ - 1, 2, 16), full(2, 16),
            half(NY, OWN), half(NY - 1, OWN), half(NR, NY, ONE), half(NR - 1, NY, ONE),
            full(NY, 16), full(ROWS_ALL, 64), full(2, 64), half(NZ, ONE), half(NZ - 1, ONE), full(64),
            pltpu.SemaphoreType.DMA((7,)),
            pltpu.SemaphoreType.DMA((8,)),
            pltpu.SemaphoreType.DMA((8,)),
            pltpu.SemaphoreType.DMA((NR // 2,)),
        ],
        compiler_params=pltpu.CompilerParams(
            collective_id=0, has_side_effects=True, vmem_limit_bytes=63 * 2**20
        ),
    )(
        page_table[0], lengths.T, steal_plan.transpose(1, 2, 0), queries[0].transpose(1, 0, 2),
        hidden_rows[0].transpose(1, 0, 2), kv_pool[0], kv_weight,
    )
    return out.transpose(1, 0, 2)[None]


def solution(mesh):
    return jax.shard_map(
        on_device,
        mesh=mesh,
        in_specs=(
            P("replica", "tensor", None, None),
            P("replica", None, "tensor"),
            P(),
            P(),
            P("replica", None, None, "tensor"),
            P("tensor", None),
            P("replica", None, None, "tensor"),
        ),
        out_specs=P("replica", None, None, "tensor"),
        check_vma=False,
    )
```

time: 50.3 us -> 45.5 us (0.905)
  Pallas kernels: 48.7 us -> 44 us
    pallas_call x1, Pallas kernels: 48.7 us -> 44 us  [on_device(): pl.pallas_call(kernel, out_shape=jax.ShapeDtypeStruct((ROWS_ALL, 2, 512),...]
where the time goes in v3:
time: 45.5 us; the launch traced here: 45.3 us
  Pallas kernels  44 us (97%)
  local copies, waits for them, and re-layouts  1.32 us (3%)
    pallas_call x1, Pallas kernels, on_device(): pl.pallas_call(kernel, out_shape=jax.ShapeDtypeStruct((ROWS_ALL, 2, 512),...  44 us
    unnamed x1, local copies, waits for them, and re-layouts  1.32 us

profile of v3, /device:TPU:1, one launch (start us, length us, event | category | flops | bytes accessed | tf_op | source)
XLA Modules:
  0.0 45.3 jit_solution(13430346208410233369)
XLA Ops:
  0.0 44.0 %shard_map.73 = bf16[7,2,512]{2,1,0:T(2,128)(2,1)} custom-call(s32[4,4]{1,0:T(4,128)} %bitcast.18, s32[4,8]{1,0:T(4,128)} %bitcast.19, s32[3,2,8]{2,1,0:T(2,128)} %bitcast.17, bf16[7,2,512]{2,1,0:T(2,128)(2,1)} %bitcast.15, bf16[7,2,512]{2,1,0:T(2,128)(2,1)} %bitcast.16, bf16[16,32,2048]{2,1,0:T(8,128)(2,1)} %bitcast.13, bf16[512,2048]{1,0:T(8,128)(2,1)} %w_hbm.1), custom_call_target="tpu_custom_call" | custom-call | tf_op jit(solution)/shard_map/pallas_call | solution.py:368
  44.0 1.3 %copy.9 = bf16[1,2,7,512]{3,1,2,0:T(2,128)(2,1)} copy(bf16[1,2,7,512]{3,1,2,0:T(2,128)(2,1)} %bitcast.14) | data formatting | bytes 28672

commit v4 on v3

--- a/solution.py
+++ b/solution.py
@@ -25,8 +25,9 @@
 F32 = jnp.float32
 BF16 = jnp.bfloat16
 INV = 1.0 / math.sqrt(HD)
-OWN = ROWS * 64 + 16
+OWN = NY * ROWS * 8 + 16
 ONE = 64 + 16
+LAST = 32 + 16
 
 
 def lanes(shape):
@@ -47,20 +48,21 @@
     return top, total, factors
 
 
-def column(x, first):
-    return jnp.concatenate([x[:, first + 4 * g:first + 4 * g + 1] for g in range(4)], axis=0)
-
-
-def merged(stat, first, parts):
-    top, total, factors = stat
-    acc = sum(column(f, first) * part.astype(F32) for f, part in zip(factors, parts))
-    return acc, column(top, first), column(total, first)
+def column(x, groups):
+    return jnp.concatenate([x[:, 4 * g:4 * g + 1] for g in range(groups)], axis=0)
+
+
+def merged(held, rows):
+    groups = rows // 16
+    top, total, factors = stat_factors([part[rows:rows + 16].astype(F32) for part in held])
+    acc = sum(column(f, groups) * part[:rows].astype(F32) for f, part in zip(factors, held))
+    return acc, column(top, groups), column(total, groups)
 
 
 def kernel(
     table_hbm, lengths_hbm, plan_hbm, q_hbm, h_hbm, pool_hbm, w_hbm, out_ref,
-    table, lengths, plan, q_ref, h_ref, pool, moved, w, qt, qz, qown, qsend, qslot,
-    fsend, frecv, fsum, fz, fresh, obo, rbo, obs, rbs, sto, macc, mst, mb, zb, fin,
+    table, lengths, plan, q_ref, h_ref, pool, moved, w, qt, qz, qyz, qown, qsend, qslot,
+    fsend, frecv, fsum, fz, fresh, obo, rbo, obs, rbs, sto, macc, mo, yb, mb, zb, fin,
     lsem, ss, rs, slot_rs,
 ):
     me = lax.axis_index("replica")
@@ -92,10 +94,10 @@
         for j in range(4):
             qt[pl.ds(s * 4 + j, ROWS_ALL, stride=8), :] = q_ref[:, s, j * HD:(j + 1) * HD].astype(F32)
     qt[56:64] = jnp.zeros((8, HD), F32)
-    qz[0] = qt[...].astype(BF16)
+    qz[0] = qt[32:64].astype(BF16)
+    qyz[0, 0] = qt[0:32].astype(BF16)
     qslot[NR - 1] = jnp.zeros((NY, 64, HD), BF16)
     sto[...] = jnp.zeros_like(sto)
-    mst[...] = jnp.zeros_like(mst)
 
     def push(src, dst, stage, peer, recv=None):
         pltpu.make_async_remote_copy(
@@ -109,12 +111,14 @@
             device_id=near(1), device_id_type=MESH,
         )
 
-    QZ, QY, QX, FY, FZ, OY, OX, OZ = range(8)
+    QZ, QY, QYZ, QX, FY, FZ, OZY, OY, OX, OZ = range(10)
 
     pl.semaphore_wait(barrier, len(peers))
 
     for o in zorder:
         push(qz.at[0], qz.at[o], QZ, near(zo=o))
+    for yo in range(1, NY):
+        push(qyz.at[0, 0], qyz.at[0, yo], QY, near(yo=yo))
 
     w_copy.wait()
     h_copy.wait()
@@ -136,11 +140,7 @@
     def by_row(r):
         return jnp.concatenate([chunk[r * 8:(r + 1) * 8] for chunk in chunks], axis=0)
 
-    for r in range(ROWS):
-        qown[0, r] = by_row(r).astype(BF16)
-    for yo in range(1, NY):
-        push(qown.at[0], qown.at[yo], QY, near(yo=yo))
-    leaving = [by_row(ROWS + e) for e in range(STEAL_IN)]
+    leaving = [by_row(e) for e in range(STEAL_IN)]
     for o in range(1, NR):
         source = (me - o + NR) % NR
         chosen = jnp.zeros((64, HD), F32)
@@ -149,6 +149,16 @@
         qsend[o - 1] = chosen.astype(BF16)
         for yo in range(NY):
             push(qsend.at[o - 1], qslot.at[o - 1, yo], QX, near(-o + NR, yo), slot_rs.at[(o - 1) // 2])
+
+    whole(qyz.at[0, 1:NY], QY).wait_recv()
+    for o in zorder:
+        push(qyz.at[0], qyz.at[o], QYZ, near(zo=o))
+    whole(frecv, FY).wait_recv()
+    for c in range(2):
+        for kind in range(2):
+            fsum[c, kind] = fsend[y, c, kind] + frecv[0, c, kind] + frecv[1, c, kind] + frecv[2, c, kind]
+    for o in zorder:
+        push(fsum.at[((z + o) % NZ) // 4], fz.at[o - 1], FZ, near(zo=o))
 
     row_id = lax.broadcasted_iota(jnp.int32, (HD, HD), 0)
     both = jnp.bitwise_and(row_id, lanes((HD, HD)))
@@ -180,7 +190,7 @@
     place = ((lane64 // PAGE) * NT + t) * PAGE + lane64 % PAGE
     blank = jnp.zeros((32, HD), BF16)
 
-    def attend(pages, a, b, query, put, put_stats, lane_a, lane_b):
+    def attend(pages, a, b, query, finish):
         (slots_a, span_a), (slots_b, span_b) = a, b
         valid = place < jnp.where(upper, span_a, span_b)
 
@@ -209,35 +219,36 @@
             values = jnp.concatenate(
                 [tokens(slots_a, (KVH + k) * HD), tokens(slots_b, (KVH + k) * HD)], axis=0
             )
-            mixed.append(jnp.dot(wide, values, preferred_element_type=F32).astype(BF16))
-        for k in range(KVH):
-            put(0, k, mixed[k][:32])
-            put(1, k, mixed[k][32:])
-        shift = (row64 % 32) // 16 * 4 + jnp.where(upper, lane_a, lane_b)
-        for c in range(KVH // 2):
-            tile = jnp.zeros((64, HD), F32)
-            for k in (2 * c, 2 * c + 1):
-                lane = lane64 - shift - 8 * (k % 2)
-                for i, piece in enumerate(tops[k] + totals[k]):
-                    tile = jnp.where(lane == i, piece, tile)
-            put_stats(0, c, tile[:16] + tile[16:32])
-            put_stats(1, c, tile[32:48] + tile[48:])
+            mixed.append(jnp.dot(wide, values, preferred_element_type=F32))
+        finish(mixed, [top + total for top, total in zip(tops, totals)])
+
+    def stamp(tile, pieces, first):
+        for i, piece in enumerate(pieces):
+            tile = jnp.where(lane64 == first + i, piece, tile)
+        return tile
 
     def pages_of(request):
         return [table[request, j] for j in range(PPD)], lengths[request, me]
 
     def own_pair(p, carry):
-        def put(i, k, value):
-            at = pl.multiple_of((2 * p + i) * 64 + (k % 2) * 32, 32)
-            obo[k // 2, pl.ds(at, 32), :] = value
-
-        def put_stats(i, c, tile):
-            sto[c] = sto[c] + tile
+        def finish(mixed, pieces):
+            at = pl.multiple_of(p * 16, 16)
+            for k in range(KVH):
+                for j in range(4):
+                    tile = jnp.concatenate([mixed[k][j * 8:j * 8 + 8], mixed[k][32 + j * 8:40 + j * 8]], axis=0)
+                    obo[k % 2 * 4 + j, pl.ds(k // 2 * 32 + at, 16), :] = tile.astype(BF16)
+            for half in range(2):
+                tile = jnp.zeros((64, HD), F32)
+                for k in range(half, KVH, 2):
+                    tile = stamp(tile, pieces[k], (k // 2 * 2 + p) * 4)
+                for j in range(4):
+                    both = jnp.concatenate([tile[j * 8:j * 8 + 8], tile[32 + j * 8:40 + j * 8]], axis=0)
+                    sto[half * 4 + j] = sto[half * 4 + j] + both
 
         def query(i, k):
-            return qown[(y - k // 2 + NY) % NY, 2 * p + i, (k % 2) * 32:(k % 2 + 1) * 32, :]
-
-        attend(pool, pages_of(2 * p), pages_of(2 * p + 1), query, put, put_stats, 32 * p, 32 * p + 16)
+            return qown[2 * p + i, k * 32:(k + 1) * 32, :]
+
+        attend(pool, pages_of(2 * p), pages_of(2 * p + 1), query, finish)
         return carry
 
     def taken(o):
@@ -247,68 +258,72 @@
             request = request + jnp.where(plan[e, 0, taker] == me, plan[e, 1, taker], 0)
         return pages_of(request)
 
-    def taken_pair(p, carry):
-        def put(i, k, value):
-            obs[2 * p + i, k // 2, (k % 2) * 32:(k % 2 + 1) * 32, :] = value
-
-        def put_stats(i, c, tile):
-            obs[2 * p + i, c, 64:80, :] = tile.astype(BF16)
+    def taken_pair(p):
+        def finish(mixed, pieces):
+            for k in range(KVH):
+                for i in range(2):
+                    obs[2 * p + i, k // 2, (k % 2) * 32:(k % 2 + 1) * 32, :] = mixed[k][i * 32:i * 32 + 32].astype(BF16)
+            for c in range(NY):
+                tile = jnp.zeros((64, HD), F32)
+                for k in (2 * c, 2 * c + 1):
+                    tile = stamp(tile, pieces[k], row64 % 32 // 16 * 4 + k % 2 * 8)
+                for i in range(2):
+                    both = tile[i * 32:i * 32 + 16] + tile[i * 32 + 16:i * 32 + 32]
+                    obs[2 * p + i, c, 64:ONE, :] = both.astype(BF16)
 
         def query(i, k):
             return qslot[2 * p + i, (y - k // 2 + NY) % NY, (k % 2) * 32:(k % 2 + 1) * 32, :]
 
-        attend(moved, taken(2 * p), taken(2 * p + 1), query, put, put_stats, 0, 0)
-        return carry
-
-    whole(qown.at[1:NY], QY).wait_recv()
-    lax.fori_loop(0, ROWS // 2, own_pair, 0)
-    for c in range(NY):
-        obo[c, ROWS * 64:OWN, :] = sto[c].astype(BF16)
-    for yo in range(1, NY):
-        push(obo.at[(y + yo) % NY], rbo.at[yo - 1], OY, near(yo=yo))
-
-    whole(frecv, FY).wait_recv()
-    for c in range(2):
-        for kind in range(2):
-            fsum[c, kind] = fsend[y, c, kind] + frecv[0, c, kind] + frecv[1, c, kind] + frecv[2, c, kind]
-    for o in zorder:
-        push(fsum.at[((z + o) % NZ) // 4], fz.at[o - 1], FZ, near(zo=o))
+        attend(moved, taken(2 * p), taken(2 * p + 1), query, finish)
 
     for p in range(NR // 2):
         whole(qslot.at[2 * p:min(2 * p + 2, NR - 1)], QX, slot_rs.at[p]).wait_recv()
-        taken_pair(p, 0)
+        taken_pair(p)
         for o in range(2 * p + 1, min(2 * p + 3, NR)):
             for yo in range(NY):
                 push(obs.at[o - 1, (y + yo) % NY], rbs.at[o - 1, yo], OX, near(o, yo))
 
-    def keep(r, acc, top, total):
-        macc[r] = acc
-        tile = jnp.zeros((64, HD), F32)
-        for i, piece in enumerate(halves(top) + halves(total)):
-            tile = jnp.where(lane64 == r // 2 * 4 + i, piece, tile)
-        mst[r % 2] = mst[r % 2] + tile
-
-    whole(rbo, OY).wait_recv()
-    held = [obo.at[y]] + [rbo.at[i] for i in range(NY - 1)]
-    stat = stat_factors([ref[ROWS * 64:OWN, :].astype(F32) for ref in held])
+    whole(qyz.at[1:NZ], QYZ).wait_recv()
+    for c in range(NT):
+        four = qyz[(z - c % NZ + NZ) % NZ, (y - c // NZ + NY) % NY].astype(F32)
+        for r in range(ROWS):
+            macc[r, c * 8:(c + 1) * 8, :] = four[r * 8:(r + 1) * 8]
     for r in range(ROWS):
-        keep(r, *merged(stat, 16 * r, [ref[r * 64:(r + 1) * 64, :] for ref in held]))
+        qown[r] = macc[r].astype(BF16)
+    lax.fori_loop(0, ROWS // 2, own_pair, 0)
+    for c in range(NZ):
+        obo[c, OWN - 16:OWN, :] = sto[c].astype(BF16)
+    for o in zorder:
+        push(obo.at[(z + o) % NZ], rbo.at[o - 1], OZY, near(zo=o))
 
     whole(rbs, OX).wait_recv()
+    marks = [jnp.zeros((64, HD), F32) for _ in range(2)]
+    taken_acc = []
     for e in range(STEAL_IN):
         o = jnp.minimum((me - plan[e, 0, me] + 2 * NR - 1) % NR, NR - 2)
-        parts = [rbs[o, i] for i in range(NY)]
-        stat = stat_factors([part[64:].astype(F32) for part in parts])
-        keep(ROWS + e, *merged(stat, 0, [part[:64] for part in parts]))
-
+        acc, top, total = merged([rbs[o, i] for i in range(NY)], 64)
+        taken_acc.append(acc)
+        marks[e % 2] = stamp(marks[e % 2], halves(top) + halves(total), e // 2 * 4)
     for c in range(NZ):
         rows = slice(c * 8, (c + 1) * 8)
-        mb[c, 0:64, :] = jnp.concatenate(
-            [macc[r, rows, :] for r in range(ROWS_ALL)] + [jnp.zeros((8, HD), F32)], axis=0
-        ).astype(BF16)
-        mb[c, 64:80, :] = jnp.concatenate([mst[0, rows, :], mst[1, rows, :]], axis=0).astype(BF16)
+        mb[c, 0:32, :] = jnp.concatenate([acc[rows] for acc in taken_acc] + [jnp.zeros((8, HD), F32)], axis=0).astype(BF16)
+        mb[c, 32:LAST, :] = jnp.concatenate([mark[rows] for mark in marks], axis=0).astype(BF16)
     for o in zorder:
         push(mb.at[(z + o) % NZ], zb.at[o - 1], OZ, near(zo=o))
+
+    whole(rbo, OZY).wait_recv()
+    acc, top, total = merged([obo[z]] + [rbo[i] for i in range(NZ - 1)], NY * 32)
+    pieces = halves(top) + halves(total)
+    lane16 = lanes((16, HD))
+    for c in range(NY):
+        mo[c, 0:32, :] = acc[c * 32:(c + 1) * 32].astype(BF16)
+        tile = jnp.zeros((16, HD), F32)
+        for p in range(2):
+            for i, piece in enumerate(pieces):
+                tile = jnp.where(lane16 == p * 4 + i, piece[c * 32 + p * 16:c * 32 + p * 16 + 16], tile)
+        mo[c, 32:LAST, :] = tile.astype(BF16)
+    for yo in range(1, NY):
+        push(mo.at[(y + yo) % NY], yb.at[yo - 1], OY, near(yo=yo))
 
     whole(fz, FZ).wait_recv()
     for kind in range(2):
@@ -328,10 +343,11 @@
     tail[1] = jnp.where(late, tail[1], MASKED)
     tail_top = jnp.maximum(tail[0], tail[1])
 
+    whole(yb, OY).wait_recv()
+    own = merged([mo[y]] + [yb[i] for i in range(NY - 1)], 32)
     whole(zb, OZ).wait_recv()
-    held = [mb.at[z]] + [zb.at[i] for i in range(NZ - 1)]
-    stat = stat_factors([ref[64:ONE, :].astype(F32) for ref in held])
-    acc, top, total = merged(stat, 0, [ref[0:64, :] for ref in held])
+    others = merged([mb[z]] + [zb[i] for i in range(NZ - 1)], 32)
+    acc, top, total = [jnp.concatenate(both, axis=0) for both in zip(own, others)]
     peak = jnp.maximum(top, tail_top)
     factor = jnp.exp(top - peak)
     first = jnp.exp(tail[0] - peak)
@@ -346,12 +362,14 @@
             out_ref[:, s, j * HD:(j + 1) * HD] = fin[pl.ds(s * 4 + j, ROWS_ALL, stride=8), :].astype(BF16)
 
     whole(qz.at[1:NZ], QZ).wait_send()
+    whole(qyz.at[0, 1:NY], QY).wait_send()
+    whole(qyz.at[1:NZ], QYZ).wait_send()
     whole(frecv, FY).wait_send()
-    whole(qown.at[1:NY], QY).wait_send()
     whole(qslot.at[0:NR - 1], QX).wait_send()
-    whole(rbo, OY).wait_send()
     whole(fz, FZ).wait_send()
+    whole(rbo, OZY).wait_send()
     whole(rbs, OX).wait_send()
+    whole(yb, OY).wait_send()
     whole(zb, OZ).wait_send()
 
 
@@ -379,13 +397,14 @@
             pltpu.VMEM((SLOTS, PAGE, width), BF16),
             pltpu.VMEM((SLOTS, PAGE, width), BF16),
             pltpu.VMEM((512, width), BF16),
-            full(64), half(NZ, 64), half(NY, ROWS, 64), half(NR - 1, 64), half(NR, NY, 64),
+            full(64), half(NZ, 32), half(NZ, NY, 32), half(ROWS, 256), half(NR - 1, 64), half(NR, NY, 64),
             full(NY, 2, 2, 16), full(NY - 1, 2, 2, 16), full(2, 2, 16), full(NZ - 1, 2, 16), full(2, 16),
-            half(NY, OWN), half(NY - 1, OWN), half(NR, NY, ONE), half(NR - 1, NY, ONE),
-            full(NY, 16), full(ROWS_ALL, 64), full(2, 64), half(NZ, ONE), half(NZ - 1, ONE), full(64),
+            half(NZ, OWN), half(NZ - 1, OWN), half(NR, NY, ONE), half(NR - 1, NY, ONE),
+            full(NZ, 16), full(ROWS, 256), half(NY, LAST), half(NY - 1, LAST), half(NZ, LAST), half(NZ - 1, LAST),
+            full(64),
             pltpu.SemaphoreType.DMA((7,)),
-            pltpu.SemaphoreType.DMA((8,)),
-            pltpu.SemaphoreType.DMA((8,)),
+            pltpu.SemaphoreType.DMA((10,)),
+            pltpu.SemaphoreType.DMA((10,)),
             pltpu.SemaphoreType.DMA((NR // 2,)),
         ],
         compiler_params=pltpu.CompilerParams(

time: 45.5 us -> 41.3 us (0.908)
  Pallas kernels: 44 us -> 39.7 us
    pallas_call x1, Pallas kernels: 44 us -> 39.7 us  [on_device(): pl.pallas_call(kernel, out_shape=jax.ShapeDtypeStruct((ROWS_ALL, 2, 512),...]
where the time goes in v4:
time: 41.3 us; the launch traced here: 41 us
  Pallas kernels  39.7 us (96%)
  local copies, waits for them, and re-layouts  1.32 us (3%)
    pallas_call x1, Pallas kernels, on_device(): pl.pallas_call(kernel, out_shape=jax.ShapeDtypeStruct((ROWS_ALL, 2, 512),...  39.7 us
    unnamed x1, local copies, waits for them, and re-layouts  1.32 us

profile of v4, /device:TPU:1, one launch (start us, length us, event | category | flops | bytes accessed | tf_op | source)
XLA Modules:
  0.0 41.0 jit_solution(3345902404806804447)
XLA Ops:
  0.0 39.7 %shard_map.73 = bf16[7,2,512]{2,1,0:T(2,128)(2,1)} custom-call(s32[4,4]{1,0:T(4,128)} %bitcast.18, s32[4,8]{1,0:T(4,128)} %bitcast.19, s32[3,2,8]{2,1,0:T(2,128)} %bitcast.17, bf16[7,2,512]{2,1,0:T(2,128)(2,1)} %bitcast.15, bf16[7,2,512]{2,1,0:T(2,128)(2,1)} %bitcast.16, bf16[16,32,2048]{2,1,0:T(8,128)(2,1)} %bitcast.13, bf16[512,2048]{1,0:T(8,128)(2,1)} %w_hbm.1), custom_call_target="tpu_custom_call" | custom-call | tf_op jit(solution)/shard_map/pallas_call | solution.py:386
  39.7 1.3 %copy.9 = bf16[1,2,7,512]{3,1,2,0:T(2,128)(2,1)} copy(bf16[1,2,7,512]{3,1,2,0:T(2,128)(2,1)} %bitcast.14) | data formatting | bytes 28672

commit v5 on v4

--- a/solution.py
+++ b/solution.py
@@ -26,7 +26,6 @@
 BF16 = jnp.bfloat16
 INV = 1.0 / math.sqrt(HD)
 OWN = NY * ROWS * 8 + 16
-ONE = 64 + 16
 LAST = 32 + 16
 
 
@@ -62,7 +61,7 @@
 def kernel(
     table_hbm, lengths_hbm, plan_hbm, q_hbm, h_hbm, pool_hbm, w_hbm, out_ref,
     table, lengths, plan, q_ref, h_ref, pool, moved, w, qt, qz, qyz, qown, qsend, qslot,
-    fsend, frecv, fsum, fz, fresh, obo, rbo, obs, rbs, sto, macc, mo, yb, mb, zb, fin,
+    fsend, frecv, fsum, fz, fresh, obo, rbo, obs, rbs, ost, rst, sto, macc, mo, yb, mb, zb, fin,
     lsem, ss, rs, slot_rs,
 ):
     me = lax.axis_index("replica")
@@ -111,7 +110,7 @@
             device_id=near(1), device_id_type=MESH,
         )
 
-    QZ, QY, QYZ, QX, FY, FZ, OZY, OY, OX, OZ = range(10)
+    QZ, QY, QYZ, QX, FY, FZ, OZY, OY, OX, OS, OZ = range(11)
 
     pl.semaphore_wait(barrier, len(peers))
 
@@ -263,13 +262,14 @@
             for k in range(KVH):
                 for i in range(2):
                     obs[2 * p + i, k // 2, (k % 2) * 32:(k % 2 + 1) * 32, :] = mixed[k][i * 32:i * 32 + 32].astype(BF16)
+            tile = jnp.zeros((64, HD), F32)
+            for k in range(KVH):
+                tile = jnp.where(lane64 == k, pieces[k][0] + pieces[k][1], tile)
+                tile = jnp.where(lane64 == KVH + k, pieces[k][2] + pieces[k][3], tile)
+            across = jnp.concatenate([tile, jnp.zeros((64, HD), F32)], axis=0).T
+            both = jnp.where(lanes((KVH, HD)) < 64, across[:KVH], pltpu.roll(across[KVH:2 * KVH], 64, 1))
             for c in range(NY):
-                tile = jnp.zeros((64, HD), F32)
-                for k in (2 * c, 2 * c + 1):
-                    tile = stamp(tile, pieces[k], row64 % 32 // 16 * 4 + k % 2 * 8)
-                for i in range(2):
-                    both = tile[i * 32:i * 32 + 16] + tile[i * 32 + 16:i * 32 + 32]
-                    obs[2 * p + i, c, 64:ONE, :] = both.astype(BF16)
+                ost[p, c] = both[2 * c:2 * c + 2]
 
         def query(i, k):
             return qslot[2 * p + i, (y - k // 2 + NY) % NY, (k % 2) * 32:(k % 2 + 1) * 32, :]
@@ -282,6 +282,7 @@
         for o in range(2 * p + 1, min(2 * p + 3, NR)):
             for yo in range(NY):
                 push(obs.at[o - 1, (y + yo) % NY], rbs.at[o - 1, yo], OX, near(o, yo))
+                push(ost.at[p, (y + yo) % NY], rst.at[o - 1, yo], OS, near(o, yo))
 
     whole(qyz.at[1:NZ], QYZ).wait_recv()
     for c in range(NT):
@@ -296,14 +297,31 @@
     for o in zorder:
         push(obo.at[(z + o) % NZ], rbo.at[o - 1], OZY, near(zo=o))
 
+    whole(rst, OS).wait_recv()
+    index = [jnp.minimum((me - plan[e, 0, me] + 2 * NR - 1) % NR, NR - 2) for e in range(STEAL_IN)]
+    row8 = lax.broadcasted_iota(jnp.int32, (8, HD), 0) // 2
+    second = jnp.zeros((8, HD), jnp.int32)
+    for e in range(STEAL_IN):
+        second = jnp.where(row8 == e, index[e] % 2, second)
+    tops = []
+    for i in range(NY):
+        tile = jnp.concatenate([rst[index[e], i] for e in range(STEAL_IN)] + [jnp.zeros((2, HD), F32)], axis=0)
+        tops.append(jnp.where(second == 1, pltpu.roll(tile, 96, 1), tile))
+    top = functools.reduce(jnp.maximum, tops)
+    factors = [jnp.exp(one - top) for one in tops]
+    total = sum(f * pltpu.roll(one, 64, 1) for f, one in zip(factors, tops))
+    down = jnp.concatenate(factors + [top, total, jnp.zeros((HD - 48, HD), F32)], axis=0).T
+
+    def down_column(i, e):
+        first = i * 8 + 2 * e
+        return jnp.concatenate([down[:32, first:first + 1], down[:32, first + 1:first + 2]], axis=0)
+
     whole(rbs, OX).wait_recv()
     marks = [jnp.zeros((64, HD), F32) for _ in range(2)]
     taken_acc = []
     for e in range(STEAL_IN):
-        o = jnp.minimum((me - plan[e, 0, me] + 2 * NR - 1) % NR, NR - 2)
-        acc, top, total = merged([rbs[o, i] for i in range(NY)], 64)
-        taken_acc.append(acc)
-        marks[e % 2] = stamp(marks[e % 2], halves(top) + halves(total), e // 2 * 4)
+        taken_acc.append(sum(down_column(i, e) * rbs[index[e], i].astype(F32) for i in range(NY)))
+        marks[e % 2] = stamp(marks[e % 2], halves(down_column(NY, e)) + halves(down_column(NY + 1, e)), e // 2 * 4)
     for c in range(NZ):
         rows = slice(c * 8, (c + 1) * 8)
         mb[c, 0:32, :] = jnp.concatenate([acc[rows] for acc in taken_acc] + [jnp.zeros((8, HD), F32)], axis=0).astype(BF16)
@@ -369,6 +387,7 @@
     whole(fz, FZ).wait_send()
     whole(rbo, OZY).wait_send()
     whole(rbs, OX).wait_send()
+    whole(rst, OS).wait_send()
     whole(yb, OY).wait_send()
     whole(zb, OZ).wait_send()
 
@@ -385,7 +404,7 @@
 
     out = pl.pallas_call(
         kernel,
-        out_shape=jax.ShapeDtypeStruct((ROWS_ALL, 2, 512), BF16),
+        out_shape=pltpu.VMEM((ROWS_ALL, 2, 512), BF16),
         in_specs=[hbm] * 7,
         out_specs=pl.BlockSpec(memory_space=pltpu.VMEM),
         scratch_shapes=[
@@ -399,12 +418,12 @@
             pltpu.VMEM((512, width), BF16),
             full(64), half(NZ, 32), half(NZ, NY, 32), half(ROWS, 256), half(NR - 1, 64), half(NR, NY, 64),
             full(NY, 2, 2, 16), full(NY - 1, 2, 2, 16), full(2, 2, 16), full(NZ - 1, 2, 16), full(2, 16),
-            half(NZ, OWN), half(NZ - 1, OWN), half(NR, NY, ONE), half(NR - 1, NY, ONE),
+            half(NZ, OWN), half(NZ - 1, OWN), half(NR, NY, 64), half(NR - 1, NY, 64), full(NR // 2, NY, 2), full(NR - 1, NY, 2),
             full(NZ, 16), full(ROWS, 256), half(NY, LAST), half(NY - 1, LAST), half(NZ, LAST), half(NZ - 1, LAST),
             full(64),
             pltpu.SemaphoreType.DMA((7,)),
-            pltpu.SemaphoreType.DMA((10,)),
-            pltpu.SemaphoreType.DMA((10,)),
+            pltpu.SemaphoreType.DMA((11,)),
+            pltpu.SemaphoreType.DMA((11,)),
             pltpu.SemaphoreType.DMA((NR // 2,)),
         ],
         compiler_params=pltpu.CompilerParams(

time: 41.3 us -> 38.8 us (0.939)
  Pallas kernels: 39.7 us -> 37.6 us
  local copies, waits for them, and re-layouts: 1.32 us -> 0.6 us
    pallas_call x1, Pallas kernels: 39.7 us -> 37.6 us  [on_device(): pl.pallas_call(kernel, out_shape=pltpu.VMEM((ROWS_ALL, 2, 512), BF16), in...]
    unnamed x1, local copies, waits for them, and re-layouts: 1.32 us -> 0.6 us
where the time goes in v5:
time: 38.8 us; the launch traced here: 38.2 us
  Pallas kernels  37.6 us (97%)
  local copies, waits for them, and re-layouts  0.6 us (2%)
    pallas_call x1, Pallas kernels, on_device(): pl.pallas_call(kernel, out_shape=pltpu.VMEM((ROWS_ALL, 2, 512), BF16), in...  37.6 us

profile of v5, /device:TPU:1, one launch (start us, length us, event | category | flops | bytes accessed | tf_op | source)
XLA Modules:
  0.0 38.2 jit_solution(12177449087231555463)
XLA Ops:
  0.0 37.6 %shard_map.73 = bf16[7,2,512]{2,1,0:T(2,128)(2,1)S(1)} custom-call(s32[4,4]{1,0:T(4,128)} %bitcast.18, s32[4,8]{1,0:T(4,128)} %bitcast.19, s32[3,2,8]{2,1,0:T(2,128)} %bitcast.17, bf16[7,2,512]{2,1,0:T(2,128)(2,1)} %bitcast.15, bf16[7,2,512]{2,1,0:T(2,128)(2,1)} %bitcast.16, bf16[16,32,2048]{2,1,0:T(8,128)(2,1)} %bitcast.14, bf16[512,2048]{1,0:T(8,128)(2,1)} %w_hbm.1), custom_call_target="tpu_custom_call" | custom-call | tf_op jit(solution)/shard_map/pallas_call | solution.py:405
  37.6 0.6 %copy.9 = bf16[1,2,7,512]{3,1,2,0:T(2,128)(2,1)} copy(bf16[1,2,7,512]{3,1,2,0:T(2,128)(2,1)S(1)} %bitcast.13) | data formatting | bytes 28672

commit v6 on v5

--- a/solution.py
+++ b/solution.py
@@ -276,7 +276,7 @@
 
         attend(moved, taken(2 * p), taken(2 * p + 1), query, finish)
 
-    for p in range(NR // 2):
+    for p in (0, 1):
         whole(qslot.at[2 * p:min(2 * p + 2, NR - 1)], QX, slot_rs.at[p]).wait_recv()
         taken_pair(p)
         for o in range(2 * p + 1, min(2 * p + 3, NR)):
@@ -296,6 +296,14 @@
         obo[c, OWN - 16:OWN, :] = sto[c].astype(BF16)
     for o in zorder:
         push(obo.at[(z + o) % NZ], rbo.at[o - 1], OZY, near(zo=o))
+
+    for p in (2, 3):
+        whole(qslot.at[2 * p:min(2 * p + 2, NR - 1)], QX, slot_rs.at[p]).wait_recv()
+        taken_pair(p)
+        for o in range(2 * p + 1, min(2 * p + 3, NR)):
+            for yo in range(NY):
+                push(obs.at[o - 1, (y + yo) % NY], rbs.at[o - 1, yo], OX, near(o, yo))
+                push(ost.at[p, (y + yo) % NY], rst.at[o - 1, yo], OS, near(o, yo))
 
     whole(rst, OS).wait_recv()
     index = [jnp.minimum((me - plan[e, 0, me] + 2 * NR - 1) % NR, NR - 2) for e in range(STEAL_IN)]

time: 38.8 us -> 38.2 us (0.985); the launches traced: 38.2 us -> 38 us
  no operation moved by 1% of the time
where the time goes in v6:
time: 38.2 us; the launch traced here: 38 us
  Pallas kernels  37.4 us (98%)
  local copies, waits for them, and re-layouts  0.6 us (2%)
    pallas_call x1, Pallas kernels, on_device(): pl.pallas_call(kernel, out_shape=pltpu.VMEM((ROWS_ALL, 2, 512), BF16), in...  37.4 us

profile of v6, /device:TPU:1, one launch (start us, length us, event | category | flops | bytes accessed | tf_op | source)
XLA Modules:
  0.0 38.0 jit_solution(8681758254504961281)
XLA Ops:
  0.0 37.4 %shard_map.73 = bf16[7,2,512]{2,1,0:T(2,128)(2,1)S(1)} custom-call(s32[4,4]{1,0:T(4,128)} %bitcast.18, s32[4,8]{1,0:T(4,128)} %bitcast.19, s32[3,2,8]{2,1,0:T(2,128)} %bitcast.17, bf16[7,2,512]{2,1,0:T(2,128)(2,1)} %bitcast.15, bf16[7,2,512]{2,1,0:T(2,128)(2,1)} %bitcast.16, bf16[16,32,2048]{2,1,0:T(8,128)(2,1)} %bitcast.14, bf16[512,2048]{1,0:T(8,128)(2,1)} %w_hbm.1), custom_call_target="tpu_custom_call" | custom-call | tf_op jit(solution)/shard_map/pallas_call | solution.py:413
  37.4 0.6 %copy.9 = bf16[1,2,7,512]{3,1,2,0:T(2,128)(2,1)} copy(bf16[1,2,7,512]{3,1,2,0:T(2,128)(2,1)S(1)} %bitcast.13) | data formatting | bytes 28672

commit v7 on v6

--- a/solution.py
+++ b/solution.py
@@ -325,15 +325,14 @@
         return jnp.concatenate([down[:32, first:first + 1], down[:32, first + 1:first + 2]], axis=0)
 
     whole(rbs, OX).wait_recv()
-    marks = [jnp.zeros((64, HD), F32) for _ in range(2)]
+    mark = jnp.zeros((64, HD), F32)
     taken_acc = []
     for e in range(STEAL_IN):
         taken_acc.append(sum(down_column(i, e) * rbs[index[e], i].astype(F32) for i in range(NY)))
-        marks[e % 2] = stamp(marks[e % 2], halves(down_column(NY, e)) + halves(down_column(NY + 1, e)), e // 2 * 4)
+        mark = stamp(mark, halves(down_column(NY, e)) + halves(down_column(NY + 1, e)), e * 4)
     for c in range(NZ):
         rows = slice(c * 8, (c + 1) * 8)
-        mb[c, 0:32, :] = jnp.concatenate([acc[rows] for acc in taken_acc] + [jnp.zeros((8, HD), F32)], axis=0).astype(BF16)
-        mb[c, 32:LAST, :] = jnp.concatenate([mark[rows] for mark in marks], axis=0).astype(BF16)
+        mb[c] = jnp.concatenate([acc[rows] for acc in taken_acc] + [mark[rows]], axis=0).astype(BF16)
     for o in zorder:
         push(mb.at[(z + o) % NZ], zb.at[o - 1], OZ, near(zo=o))
 
@@ -372,7 +371,14 @@
     whole(yb, OY).wait_recv()
     own = merged([mo[y]] + [yb[i] for i in range(NY - 1)], 32)
     whole(zb, OZ).wait_recv()
-    others = merged([mb[z]] + [zb[i] for i in range(NZ - 1)], 32)
+    held = [mb[z].astype(F32)] + [zb[i].astype(F32) for i in range(NZ - 1)]
+    top, total, factors = stat_factors([part[24:32] for part in held])
+    none = jnp.zeros((8, 1), F32)
+
+    def by_entry(x):
+        return jnp.concatenate([x[:, 4 * e:4 * e + 1] for e in range(STEAL_IN)] + [none], axis=0)
+
+    others = sum(by_entry(f) * part for f, part in zip(factors, held)), by_entry(top), by_entry(total)
     acc, top, total = [jnp.concatenate(both, axis=0) for both in zip(own, others)]
     peak = jnp.maximum(top, tail_top)
     factor = jnp.exp(top - peak)
@@ -427,7 +433,7 @@
             full(64), half(NZ, 32), half(NZ, NY, 32), half(ROWS, 256), half(NR - 1, 64), half(NR, NY, 64),
             full(NY, 2, 2, 16), full(NY - 1, 2, 2, 16), full(2, 2, 16), full(NZ - 1, 2, 16), full(2, 16),
             half(NZ, OWN), half(NZ - 1, OWN), half(NR, NY, 64), half(NR - 1, NY, 64), full(NR // 2, NY, 2), full(NR - 1, NY, 2),
-            full(NZ, 16), full(ROWS, 256), half(NY, LAST), half(NY - 1, LAST), half(NZ, LAST), half(NZ - 1, LAST),
+            full(NZ, 16), full(ROWS, 256), half(NY, LAST), half(NY - 1, LAST), half(NZ, 32), half(NZ - 1, 32),
             full(64),
             pltpu.SemaphoreType.DMA((7,)),
             pltpu.SemaphoreType.DMA((11,)),

time: 38.2 us -> 38.1 us (level)
  no operation moved by 1% of the time
where the time goes in v7:
time: 38.1 us; the launch traced here: 38 us
  Pallas kernels  37.4 us (98%)
  local copies, waits for them, and re-layouts  0.6 us (2%)
    pallas_call x1, Pallas kernels, on_device(): pl.pallas_call(kernel, out_shape=pltpu.VMEM((ROWS_ALL, 2, 512), BF16), in...  37.4 us

profile of v7, /device:TPU:1, one launch (start us, length us, event | category | flops | bytes accessed | tf_op | source)
XLA Modules:
  0.0 38.0 jit_solution(13862213084517470750)
XLA Ops:
  0.0 37.4 %shard_map.73 = bf16[7,2,512]{2,1,0:T(2,128)(2,1)S(1)} custom-call(s32[4,4]{1,0:T(4,128)} %bitcast.18, s32[4,8]{1,0:T(4,128)} %bitcast.19, s32[3,2,8]{2,1,0:T(2,128)} %bitcast.17, bf16[7,2,512]{2,1,0:T(2,128)(2,1)} %bitcast.15, bf16[7,2,512]{2,1,0:T(2,128)(2,1)} %bitcast.16, bf16[16,32,2048]{2,1,0:T(8,128)(2,1)} %bitcast.14, bf16[512,2048]{1,0:T(8,128)(2,1)} %w_hbm.1), custom_call_target="tpu_custom_call" | custom-call | tf_op jit(solution)/shard_map/pallas_call | solution.py:419
  37.4 0.6 %copy.9 = bf16[1,2,7,512]{3,1,2,0:T(2,128)(2,1)} copy(bf16[1,2,7,512]{3,1,2,0:T(2,128)(2,1)S(1)} %bitcast.13) | data formatting | bytes 28672
